TPU v7x, 512 devices: a whole 4x8x8 slice. The times are simulated.
512 devices in a mesh: group: 8 (over x, core), shard: 64 (over z, y).
Axes of the slice: x: 4, y: 8, z: 8, core: 2. Of those that a mesh axis runs over, the one named last changes fastest.
Arguments:
- queries: bfloat16 [4096, 768], P(('group', 'shard'))
- positives: int32 [4096], P(('group', 'shard')), may hold values from 0 to 196607
- cache: bfloat16 [196608, 768], P('shard')
- fresh: bfloat16 [8192, 768], P(('group', 'shard')), may hold values from -12 to 12
- slots: int32 [8192], P(('group', 'shard')), may hold values from 0 to 196607, as said below
Outputs:
- query_grad: float32 [4096, 768], P(('group', 'shard'))
- loss: float32 [4096], P(('group', 'shard'))
Inputs may be any that keep to these rules, and one draw needn't show every extreme that they name: All 8192 slots are distinct; the fresh passage in row r has its slot among cache rows s * 3072 to (s + 1) * 3072 - 1, where s = (r // 16) % (the size of shard); in each such range rows s * 3072 and (s + 1) * 3072 - 1 are overwritten.
All inputs are finite; a program needn't handle non-finite values.
Results may differ from a plain program's by a relative error of at most 0.004.
Values may be sent and summed in bfloat16 or wider, within the bound.
No kernel may reach another device: no remote copies, remote signals or barrier semaphores. Data moves between devices by JAX's collectives and lax.ppermute only.
A program may use at most 128 MiB of HBM per device.

v0:
```python
import math

import jax
import jax.numpy as jnp
from jax import lax
from jax.sharding import PartitionSpec as P


def per_device(queries, positives, cache, fresh, slots):
    row_count = cache.shape[0]
    score_scale = 1.0 / math.sqrt(cache.shape[1])
    first_row = lax.axis_index("shard") * row_count
    group_rows, group_pos = (
        lax.all_gather(queries, "shard", axis=0, tiled=True),
        lax.all_gather(positives, "shard", axis=0, tiled=True),
    )
    new_rows, new_slots = (
        lax.all_gather(fresh, "group", axis=0, tiled=True),
        lax.all_gather(slots, "group", axis=0, tiled=True),
    )
    local_new = new_slots - first_row
    pos_local = group_pos - first_row
    is_owned = (pos_local >= 0) & (pos_local < row_count)
    safe_pos = jnp.clip(pos_local, 0, row_count - 1)
    updated = cache.at[local_new].set(new_rows)
    scores = jnp.dot(group_rows, updated.T, preferred_element_type=jnp.float32) * score_scale
    local_top = jnp.max(scores, axis=1)
    local_total = jnp.sum(jnp.exp(scores - local_top[:, None]), axis=1)
    pos_score = jnp.where(
        is_owned, jnp.take_along_axis(scores, safe_pos[:, None], axis=1)[:, 0], 0.0
    )
    pos_rows = jnp.where(is_owned[:, None], updated[safe_pos].astype(jnp.float32), 0.0)
    row_top = lax.pmax(local_top, "shard")
    row_total, pos_total = lax.psum(
        (local_total * jnp.exp(local_top - row_top), pos_score), "shard"
    )
    weights = (jnp.exp(scores - row_top[:, None]) / row_total[:, None]).astype(jnp.bfloat16)
    own_count = queries.shape[0]
    target_rows = lax.slice_in_dim(pos_rows, 0, own_count * lax.axis_size("shard"), axis=0)
    partial_grad = lax.psum_scatter(
        jnp.dot(weights, updated, preferred_element_type=jnp.float32) - target_rows,
        "shard",
        scatter_dimension=0,
        tiled=True,
    )
    query_grad = partial_grad * score_scale
    all_loss = jnp.log(row_total) + row_top - pos_total
    own_loss = lax.dynamic_slice_in_dim(all_loss, lax.axis_index("shard") * own_count, own_count, 0)
    return (query_grad, own_loss)


def solution(mesh):
    return jax.shard_map(
        per_device,
        mesh=mesh,
        in_specs=(
            P(("group", "shard"), None),
            P(("group", "shard")),
            P("shard", None),
            P(("group", "shard"), None),
            P(("group", "shard")),
        ),
        out_specs=(P(("group", "shard"), None), P(("group", "shard"))),
        check_vma=False,
    )
```

profile of v0, /device:TPU:6, one launch (start us, length us, event | category | flops | bytes accessed | tf_op | source)
XLA Modules:
  0.0 610.2 jit_solution(11029056963247371835)
XLA Ops:
  7.2 0.0 copy-start.2
  7.2 0.0 copy-start.1
  7.2 0.0 copy-start.4
  7.2 0.0 all-reduce.6.cloned.1.call-start
  7.2 4.7 copy.12
  12.0 1.3 dynamic-slice
  13.9 0.0 copy-done.4
  13.9 0.2 dynamic-update-slice
  14.2 12.3 %all-reduce = s32[128]{0:T(128)S(1)} all-reduce(s32[128]{0:T(128)S(1)} %dynamic-update-slice), channel_id=1, replica_groups=mesh['group'=8,'shard'=64] {'group'}, use_global_device_ids=true, to_apply=%add | all-reduce | flops 128 | bytes 1024
  26.5 0.0 copy-done.1
  26.5 12.8 %all_gather.13 = bf16[128,768]{1,0:T(8,128)(2,1)S(1)} all-gather(bf16[16,768]{1,0:T(8,128)(2,1)S(1)} %copy-done.1), channel_id=1, replica_groups=mesh['group'=8,'shard'=64] {'group'}, dimensions={0}, use_global_device_ids=true | all-gather | bytes 221184 | tf_op jit(solution)/shard_map/all_gather | solution.py:18
  39.3 0.0 copy-done.2
  39.3 52.5 %all_gather.14 = bf16[512,768]{1,0:T(8,128)(2,1)S(1)} all-gather(bf16[8,768]{1,0:T(8,128)(2,1)S(1)} %copy-done.2), channel_id=1, replica_groups=mesh['group'=8,'shard'=64] {'shard'}, dimensions={0}, use_global_device_ids=true | all-gather | bytes 798720 | tf_op jit(solution)/shard_map/all_gather | solution.py:14
  91.8 6.5 %scatter_fusion = bf16[3072,768]{1,0:T(8,128)(2,1)} fusion(bf16[3072,768]{1,0:T(8,128)(2,1)} %copy.12, s32[128]{0:T(128)S(1)} %compare_select_fusion.1, bf16[128,768]{1,0:T(8,128)(2,1)S(1)} %all_gather.13), kind=kCustom, calls=%fused_computation.2 | custom fusion | bytes 590336 | tf_op jit(solution)/shard_map/scatter | solution.py:25
  98.3 4.7 fusion.5
  102.9 0.0 copy-start
  102.9 3.9 multiply_bitcast_fusion
  106.8 0.0 copy-start.3
  106.8 0.0 copy-start.5
  106.8 0.7 copy-done
  107.5 1.1 exponential_reduce_fusion
  108.6 140.7 %pmax.7 = f32[512]{0:T(512)S(1)} all-reduce(f32[512]{0:T(512)S(1)} %get-tuple-element.7), channel_id=1, replica_groups=mesh['group'=8,'shard'=64] {'shard'}, use_global_device_ids=true, to_apply=%region_2.3 | all-reduce | flops 512 | bytes 4096 | tf_op jit(solution)/shard_map/pmax | solution.py:33
  249.3 0.0 copy-done.3
  249.3 0.6 fusion.4
  250.6 0.0 copy-done.5
  250.6 0.2 dynamic-update-slice.1
  250.8 18.2 %all-reduce.1 = s32[512]{0:T(512)S(1)} all-reduce(s32[512]{0:T(512)S(1)} %dynamic-update-slice.1), channel_id=1, replica_groups=mesh['group'=8,'shard'=64] {'shard'}, use_global_device_ids=true, to_apply=%add.1 | all-reduce | flops 512 | bytes 4096
  269.1 22.5 %gather_fusion.1 = f32[512]{0:T(512)S(1)} fusion(f32[512,3072]{0,1:T(8,128)} %get-tuple-element.6, s32[512]{0:T(512)S(1)} %bitcast.17), kind=kCustom, calls=%fused_computation.1 | custom fusion | bytes 8192 | tf_op jit(solution)/shard_map/jit(take_along_axis)/gather | solution.py:30
  291.7 5.3 gather_fusion
  297.0 144.0 %all-reduce.3 = (f32[512]{0:T(512)S(1)}, f32[512]{0:T(512)S(1)}) all-reduce(f32[512]{0:T(512)S(1)} %exponential_multiply_fusion, f32[512]{0:T(512)S(1)} %get-tuple-element.4), channel_id=1, replica_groups=mesh['group'=8,'shard'=64] {'shard'}, use_global_device_ids=true, to_apply=%region_4.5 | all-reduce | flops 1024 | bytes 8192 | tf_op jit(solution)/shard_map/psum | solution.py:34
  441.0 8.1 %select_subtract_fusion = f32[512,768]{1,0:T(8,128)} fusion(bf16[512,768]{1,0:T(8,128)(2,1)S(1)} %gather_fusion, bf16[3072,768]{1,0:T(8,128)(2,1)} %scatter_fusion, f32[512]{0:T(512)S(1)} %get-tuple-element.2, f32[512]{0:T(512)S(1)} %pmax.7, pred[512]{0:T(512)(128)(4,1)S(1)} %get-tuple-element.5, f32[3072,512]{1,0:T(8,128)} %copy-done), kind=kOutput, calls=%fused_computation.8 | convolution fusion | flops 2423390208 | bytes 13373952 | tf_op jit(solution)/shard_map/dot_general | solution.py:41
  449.1 0.0 all-reduce.6.cloned.1.call-update
  449.1 0.6 dynamic_slice.3
  450.3 151.7 %all-reduce.6.cloned.1.call-done = f32[512,768]{1,0:T(8,128)} async-done(((f32[512,768]{1,0:T(8,128)}), f32[512,768]{1,0:T(8,128)}) %all-reduce.6.cloned.1.call-update) | async-done | bytes 1572880
  602.0 1.3 dynamic-slice_multiply_fusion
  (11 shorter events, 0.1 us)
Async XLA Ops:
  7.2 32.1 %copy-start.2 = (bf16[8,768]{1,0:T(8,128)(2,1)S(1)}, bf16[8,768]{1,0:T(8,128)(2,1)}, u32[]{:S(2)}) copy-start(bf16[8,768]{1,0:T(8,128)(2,1)} %param.5) | copy-start | bytes 36868
  7.2 19.3 %copy-start.1 = (bf16[16,768]{1,0:T(8,128)(2,1)S(1)}, bf16[16,768]{1,0:T(8,128)(2,1)}, u32[]{:S(2)}) copy-start(bf16[16,768]{1,0:T(8,128)(2,1)} %param.8) | copy-start | bytes 73732
  7.2 6.7 %copy-start.4 = (s32[16]{0:T(128)S(1)}, s32[16]{0:T(128)}, u32[]{:S(2)}) copy-start(s32[16]{0:T(128)} %param.9) | copy-start | bytes 196
  7.2 594.8 %all-reduce.6.cloned.1.call-start = ((), (), s32[]{:S(2)}) async-start(), calls=%async_computation | async-start | bytes 3145728
  102.9 4.6 copy-start
  106.8 142.5 %copy-start.3 = (u32[512]{0:T(512)S(1)}, u32[512]{0:T(512)}, u32[]{:S(2)}) copy-start(u32[512]{0:T(512)} %constant.62) | copy-start | bytes 6148
  106.8 143.7 %copy-start.5 = (s32[8]{0:T(128)S(1)}, s32[8]{0:T(128)}, u32[]{:S(2)}) copy-start(s32[8]{0:T(128)} %param.6) | copy-start | bytes 100
Sparse Core Ops, SparseCore 0:
  449.2 152.7 all-reduce.5
where the time goes:
time: 611 us; the launch traced here: 610 us
  blocking collectives  380 us (62%)
  waiting for transfers between devices  152 us (25%)
  local copies, waits for them, and re-layouts  42.7 us (7%)
  between operations  16.1 us (3%)
  matrix products  12.7 us (2%)
  other arithmetic  6.43 us (1%)
    unnamed x2, waiting for transfers between devices  152 us
    psum x1, blocking collectives, per_device(): lax.psum((local_total * jnp.exp(local_top - row_top), pos_score), 'shard')  144 us
    pmax x1, blocking collectives, per_device(): row_top = lax.pmax(local_top, 'shard')  141 us
    all_gather x1, blocking collectives, per_device(): lax.all_gather(queries, 'shard', axis=0, tiled=True)  52.5 us
    unnamed x2, blocking collectives  30.5 us
    gather x1, local copies, waits for them, and re-layouts, per_device(): jnp.take_along_axis(scores, safe_pos[:, None], axis=1)[:, 0]  22.5 us
    all_gather x1, blocking collectives, per_device(): lax.all_gather(fresh, 'group', axis=0, tiled=True)  12.8 us
  transfers between devices with their start and end apart: 1, of which 1 were waited for; matrix products, arithmetic and copies ran while one was open for 0% of the time, Pallas kernels for 0%

commit v1 on v0

v1 whole, which is shorter than its diff:
```python
import functools
import math

import jax
import jax.numpy as jnp
from jax import lax
from jax.experimental import pallas as pl
from jax.experimental.pallas import tpu as pltpu
from jax.sharding import PartitionSpec as P

LANES = 128
LOG2E = math.log2(math.e)


def with_digits(rows, numbers, digits):
    parts = jnp.stack([(numbers >> (8 * k)) & 255 for k in range(digits)], axis=1)
    tail = jnp.pad(parts.astype(rows.dtype), ((0, 0), (0, LANES - digits)))
    return jnp.concatenate([rows, tail], axis=1)


def split3(x):
    hi = x.astype(jnp.bfloat16)
    rest = x - hi.astype(jnp.float32)
    mid = rest.astype(jnp.bfloat16)
    low = (rest - mid.astype(jnp.float32)).astype(jnp.bfloat16)
    return hi, mid, low


def partial_kernel(chunk, first_ref, got_ref, table_ref, out_ref, scores_ref):
    count, width = got_ref.shape
    depth = width - LANES
    rows = table_ref.shape[0]
    to_log2 = LOG2E / math.sqrt(depth)
    queries = got_ref[:, :depth]
    digits = got_ref[:, depth:].astype(jnp.float32)
    lane = lax.broadcasted_iota(jnp.int32, (1, LANES), 1)
    weight = jnp.where(lane == 0, 1.0, jnp.where(lane == 1, 256.0, jnp.where(lane == 2, 65536.0, 0.0)))
    where = jnp.sum(digits * weight, axis=1, keepdims=True) - first_ref[0].astype(jnp.float32)
    where = where.astype(jnp.int32)

    top = jnp.full((count, LANES), -jnp.inf, jnp.float32)
    for start in range(0, rows, chunk):
        part = lax.dot_general(
            queries, table_ref[start:start + chunk, :], (((1,), (1,)), ((), ())),
            preferred_element_type=jnp.float32,
        )
        scores_ref[:, start:start + chunk] = part
        for at in range(0, chunk, LANES):
            top = jnp.maximum(top, part[:, at:at + LANES])
    top = jnp.max(top, axis=1, keepdims=True) * to_log2

    total = jnp.zeros((count, LANES), jnp.float32)
    summed = jnp.zeros((count, depth), jnp.float32)
    picked = jnp.zeros((count, depth), jnp.float32)
    column = lax.broadcasted_iota(jnp.int32, (count, chunk), 1)
    for start in range(0, rows, chunk):
        weights = jnp.exp2(scores_ref[:, start:start + chunk] * to_log2 - top)
        for at in range(0, chunk, LANES):
            total = total + weights[:, at:at + LANES]
        block = table_ref[start:start + chunk, :]
        summed = summed + jnp.dot(weights.astype(jnp.bfloat16), block, preferred_element_type=jnp.float32)
        chosen = jnp.where(column == where - start, 1.0, 0.0).astype(jnp.bfloat16)
        picked = picked + jnp.dot(chosen, block, preferred_element_type=jnp.float32)
    total = jnp.sum(total, axis=1, keepdims=True)
    out_ref[:, :depth] = (summed / total).astype(jnp.bfloat16)
    out_ref[:, depth:2 * depth] = picked.astype(jnp.bfloat16)
    hi, mid, low = split3(jnp.broadcast_to(top + jnp.log2(total), (count, LANES)))
    zero = jnp.zeros((count, LANES), jnp.bfloat16)
    out_ref[:, 2 * depth:] = jnp.where(lane == 0, hi, jnp.where(lane == 1, mid, jnp.where(lane == 2, low, zero)))


def combine_kernel(got_ref, own_ref, grad_ref, loss_ref):
    sources, own, width = got_ref.shape
    depth = own_ref.shape[1]
    scale = 1.0 / math.sqrt(depth)
    tail = got_ref[:, :, 2 * depth:].astype(jnp.float32)
    logs = jnp.sum(tail, axis=2, keepdims=True)
    top = jnp.max(logs, axis=0, keepdims=True)
    share = jnp.exp2(logs - top)
    total = jnp.sum(share, axis=0)
    summed = jnp.sum(got_ref[:, :, :depth].astype(jnp.float32) * share, axis=0)
    positive = jnp.sum(got_ref[:, :, depth:2 * depth].astype(jnp.float32), axis=0)
    grad_ref[...] = (summed / total - positive) * scale
    pos_score = jnp.sum(own_ref[...].astype(jnp.float32) * positive, axis=1, keepdims=True) * scale
    loss = (top[0] + jnp.log2(total)) * (1.0 / LOG2E) - pos_score
    loss_ref[...] = jnp.broadcast_to(loss, (own, LANES))


def per_device(queries, positives, cache, fresh, slots):
    own, depth = queries.shape
    rows = cache.shape[0]
    shards = lax.axis_size("shard")
    groups = lax.axis_size("group")
    first = lax.axis_index("shard") * rows

    sent = with_digits(queries, positives, 3)
    got = lax.all_to_all(
        jnp.broadcast_to(sent[None], (shards,) + sent.shape), "shard", 0, 0
    ).reshape(shards * own, depth + LANES)

    new = with_digits(fresh, slots - first, 2)
    for bit in (1, 4, 2):
        other = lax.ppermute(new, "group", [(i, i ^ bit) for i in range(groups)])
        new = jnp.concatenate([new, other], axis=0)
    at = new[:, depth:depth + 2].astype(jnp.int32)
    table = cache.at[at[:, 0] + 256 * at[:, 1]].set(
        new[:, :depth], unique_indices=True, mode="promise_in_bounds"
    )

    vmem = pl.BlockSpec(memory_space=pltpu.VMEM)
    width = 2 * depth + LANES
    count = shards * own
    part = pl.pallas_call(
        functools.partial(partial_kernel, 512),
        out_shape=jax.ShapeDtypeStruct((count, width), jnp.bfloat16),
        in_specs=[pl.BlockSpec(memory_space=pltpu.SMEM), vmem, vmem],
        out_specs=vmem,
        scratch_shapes=[pltpu.VMEM((count, rows), jnp.float32)],
        compiler_params=pltpu.CompilerParams(vmem_limit_bytes=48 * 1024 * 1024),
        cost_estimate=pl.CostEstimate(
            flops=6 * count * rows * depth, bytes_accessed=2 * rows * depth, transcendentals=count * rows
        ),
    )(first.reshape(1).astype(jnp.int32), got, table)

    back = lax.all_to_all(part.reshape(shards, own, width), "shard", 0, 0)
    grad, loss = pl.pallas_call(
        combine_kernel,
        out_shape=(
            jax.ShapeDtypeStruct((own, depth), jnp.float32),
            jax.ShapeDtypeStruct((own, LANES), jnp.float32),
        ),
        in_specs=[vmem, vmem],
        out_specs=(vmem, vmem),
        compiler_params=pltpu.CompilerParams(vmem_limit_bytes=32 * 1024 * 1024),
    )(back, queries)
    return grad, loss[:, 0]


def solution(mesh):
    return jax.shard_map(
        per_device,
        mesh=mesh,
        in_specs=(
            P(("group", "shard"), None),
            P(("group", "shard")),
            P("shard", None),
            P(("group", "shard"), None),
            P(("group", "shard")),
        ),
        out_specs=(P(("group", "shard"), None), P(("group", "shard"))),
        check_vma=False,
    )
```

time: 611 us -> 116 us (0.19)
  blocking collectives: 380 us -> 52.4 us
  waiting for transfers between devices: 152 us -> 12.1 us
  local copies, waits for them, and re-layouts: 42.7 us -> 6.67 us
  starting transfers between devices: 0.04 us -> 24.5 us
  between operations: 16.1 us -> 0.75 us
  matrix products: 12.7 us -> 0 us
  Pallas kernels: 0 us -> 12 us
    unnamed x2 -> x0, waiting for transfers between devices: 152 us -> none
    psum x1 -> x0, blocking collectives: 144 us -> none  [per_device(): lax.psum((local_total * jnp.exp(local_top - row_top), pos_score), 'shard')]
    pmax x1 -> x0, blocking collectives: 141 us -> none  [per_device(): row_top = lax.pmax(local_top, 'shard')]
    all_gather x2 -> x0, blocking collectives: 65.3 us -> none  [the longest x1 52.5 us: per_device(): lax.all_gather(queries, 'shard', axis=0, tiled=True)]
    all_to_all x0 -> x1, blocking collectives: none -> 52.4 us  [per_device(): back = lax.all_to_all(part.reshape(shards, own, width), 'shard', 0, 0)]
    unnamed x2 -> x0, blocking collectives: 30.5 us -> none
    gather x2 -> x0, local copies, waits for them, and re-layouts: 27.9 us -> none  [the longest x1 22.5 us: per_device(): jnp.take_along_axis(scores, safe_pos[:, None], axis=1)[:, 0]]
    all_to_all x0 -> x1, starting transfers between devices: none -> 16.6 us  [per_device(): lax.all_to_all(jnp.broadcast_to(sent[None], (shards,) + sent.shape), 'sha...]
  transfers between devices with their start and end apart: 1 -> 4, of which waited for: 1 -> 4; matrix products, arithmetic and copies ran while one was open for 0% -> 6% of each run, Pallas kernels for 0% -> 0%
where the time goes in v1:
time: 116 us; the launch traced here: 115 us
  blocking collectives  52.4 us (45%)
  starting transfers between devices  24.5 us (21%)
  waiting for transfers between devices  12.1 us (10%)
  Pallas kernels  12 us (10%)
  other arithmetic  6.77 us (6%)
  local copies, waits for them, and re-layouts  6.67 us (6%)
    all_to_all x1, blocking collectives, per_device(): back = lax.all_to_all(part.reshape(shards, own, width), 'shard', 0, 0)  52.4 us
    all_to_all x1, starting transfers between devices, per_device(): lax.all_to_all(jnp.broadcast_to(sent[None], (shards,) + sent.shape), 'sha...  16.6 us
    pallas_call x1, Pallas kernels, per_device(): pl.pallas_call(functools.partial(partial_kernel, 512), out_shape=jax.Shap...  10.9 us
    ppermute x3, waiting for transfers between devices, per_device(): other = lax.ppermute(new, 'group', [(i, i ^ bit) for i in range(groups)])  9.36 us
    ppermute x3, starting transfers between devices, per_device(): other = lax.ppermute(new, 'group', [(i, i ^ bit) for i in range(groups)])  7.96 us
    scatter x1, other arithmetic, per_device(): cache.at[at[:, 0] + 256 * at[:, 1]]  6.52 us
    unnamed x11, local copies, waits for them, and re-layouts  4.99 us
    all_to_all x1, waiting for transfers between devices, per_device(): lax.all_to_all(jnp.broadcast_to(sent[None], (shards,) + sent.shape), 'sha...  2.76 us
  transfers between devices with their start and end apart: 4, of which 4 were waited for; matrix products, arithmetic and copies ran while one was open for 6% of the time, Pallas kernels for 0%

profile of v1, /device:TPU:6, one launch (start us, length us, event | category | flops | bytes accessed | tf_op | source)
XLA Modules:
  0.0 115.2 jit_solution(8150503556458195305)
XLA Ops:
  0.6 0.0 copy-start.2
  0.6 0.0 copy-start
  0.7 0.0 copy-start.3
  0.7 0.0 copy-start.1
  0.7 4.8 %copy.15 = bf16[3072,768]{1,0:T(8,128)(2,1)} copy(bf16[3072,768]{1,0:T(8,128)(2,1)} %param.7) | data formatting | bytes 9437184
  5.5 0.0 copy-done.2
  5.5 0.1 copy.11
  5.6 0.0 copy-done
  5.6 1.0 broadcast_in_dim.2
  6.6 16.6 %all-to-all-start = ((bf16[64,8,896]{2,1,0:T(8,128)(2,1)}), bf16[64,8,896]{2,1,0:T(8,128)(2,1)S(1)}, u32[]{:S(2)}, u32[]{:S(2)}) async-start(bf16[64,8,896]{2,1,0:T(8,128)(2,1)} %broadcast_in_dim.2), calls=%async_computation | async-start | bytes 1835008 | tf_op jit(solution)/shard_map/all_to_all | solution.py:97
  23.2 0.0 copy-done.3
  23.3 0.1 copy.12
  23.4 0.0 copy-done.1
  23.4 1.9 %collective-permute-start = (bf16[16,896]{1,0:T(8,128)(2,1)S(1)}, bf16[16,896]{1,0:T(8,128)(2,1)S(1)}, u32[]{:S(2)}, u32[]{:S(2)}) collective-permute-start(bf16[16,896]{1,0:T(8,128)(2,1)S(1)} %pad_maximum_fusion.10), channel_id=1, source_target_pairs={{0,64},{64,0},{128,192},{192,128},{256,320},{320,256},{384,448},{4... | collective-permute-start | bytes 86024 | tf_op jit(solution)/shard_map/ppermute | solution.py:103
  25.3 1.2 %collective-permute-done = bf16[16,896]{1,0:T(8,128)(2,1)S(1)} collective-permute-done((bf16[16,896]{1,0:T(8,128)(2,1)S(1)}, bf16[16,896]{1,0:T(8,128)(2,1)S(1)}, u32[]{:S(2)}, u32[]{:S(2)}) %collective-permute-start) | collective-permute-done | bytes 28704 | tf_op jit(solution)/shard_map/ppermute | solution.py:103
  26.5 3.3 %collective-permute-start.1 = (bf16[32,896]{1,0:T(8,128)(2,1)S(1)}, bf16[32,896]{1,0:T(8,128)(2,1)S(1)}, u32[]{:S(2)}, u32[]{:S(2)}) collective-permute-start(bf16[32,896]{1,0:T(8,128)(2,1)S(1)} %pad_maximum_fusion.9), channel_id=1, source_target_pairs={{0,256},{64,320},{128,384},{192,448},{256,0},{320,64},{384,128},{4... | collective-permute-start | bytes 172040 | tf_op jit(solution)/shard_map/ppermute | solution.py:103
  29.8 4.3 %collective-permute-done.1 = bf16[32,896]{1,0:T(8,128)(2,1)S(1)} collective-permute-done((bf16[32,896]{1,0:T(8,128)(2,1)S(1)}, bf16[32,896]{1,0:T(8,128)(2,1)S(1)}, u32[]{:S(2)}, u32[]{:S(2)}) %collective-permute-start.1) | collective-permute-done | bytes 57376 | tf_op jit(solution)/shard_map/ppermute | solution.py:103
  34.1 2.7 %collective-permute-start.2 = (bf16[64,896]{1,0:T(8,128)(2,1)S(1)}, bf16[64,896]{1,0:T(8,128)(2,1)S(1)}, u32[]{:S(2)}, u32[]{:S(2)}) collective-permute-start(bf16[64,896]{1,0:T(8,128)(2,1)S(1)} %pad_maximum_fusion.8), channel_id=1, source_target_pairs={{0,128},{64,192},{128,0},{192,64},{256,384},{320,448},{384,256},{4... | collective-permute-start | bytes 344072 | tf_op jit(solution)/shard_map/ppermute | solution.py:103
  36.8 3.9 %collective-permute-done.2 = bf16[64,896]{1,0:T(8,128)(2,1)S(1)} collective-permute-done((bf16[64,896]{1,0:T(8,128)(2,1)S(1)}, bf16[64,896]{1,0:T(8,128)(2,1)S(1)}, u32[]{:S(2)}, u32[]{:S(2)}) %collective-permute-start.2) | collective-permute-done | bytes 114720 | tf_op jit(solution)/shard_map/ppermute | solution.py:103
  40.8 0.2 fusion.2
  40.9 6.5 %scatter_custom_fusion.table_ref = bf16[3072,768]{1,0:T(8,128)(2,1)} fusion(bf16[3072,768]{1,0:T(8,128)(2,1)} %copy.15, s32[128]{0:T(128)S(1)} %fusion.2, bf16[64,896]{1,0:T(8,128)(2,1)S(1)} %collective-permute-done.2, bf16[]{:T(256)} %constant.34, bf16[32,896]{1,0:T(8,128)(2,1)S(1)} %collective-permute-done.1, ...), kind=kCustom, calls=%fused_computation.2 | custom fusion | flops 983040 | bytes 4948480 | tf_op jit(solution)/shard_map/scatter | solution.py:106
  47.5 2.8 %all-to-all-done = bf16[64,8,896]{2,1,0:T(8,128)(2,1)S(1)} async-done(((bf16[64,8,896]{2,1,0:T(8,128)(2,1)}), bf16[64,8,896]{2,1,0:T(8,128)(2,1)S(1)}, u32[]{:S(2)}, u32[]{:S(2)}) %all-to-all-start) | async-done | bytes 917536 | tf_op jit(solution)/shard_map/all_to_all | solution.py:97
  50.2 10.9 %shard_map.68 = bf16[512,1664]{1,0:T(8,128)(2,1)S(1)} custom-call(s32[1]{0:T(128)} %bitcast.first_ref, bf16[512,896]{1,0:T(8,128)(2,1)S(1)} %bitcast.14, bf16[3072,768]{1,0:T(8,128)(2,1)} %scatter_custom_fusion.table_ref), custom_call_target="tpu_custom_call" | custom-call | flops 7247757312 | bytes 4718592 | tf_op jit(solution)/shard_map/pallas_call | solution.py:113
  61.2 52.4 %all_to_all.10.got_ref = bf16[64,8,1664]{2,1,0:T(8,128)(2,1)S(1)} all-to-all(bf16[64,8,1664]{2,1,0:T(8,128)(2,1)S(1)} %bitcast.13), channel_id=1, replica_groups=mesh['group'=8,'shard'=64] {'shard'}, dimensions={0} | all-to-all | bytes 3407872 | tf_op jit(solution)/shard_map/all_to_all | solution.py:125
  113.5 1.0 shard_map.69
  114.6 0.6 slice_reduce_fusion
  (10 shorter events, 0.1 us)
Async XLA Ops:
  0.6 4.8 %copy-start.2 = (s32[8]{0:T(128)S(1)}, s32[8]{0:T(128)}, u32[]{:S(2)}) copy-start(s32[8]{0:T(128)} %param.6) | copy-start | bytes 100
  0.6 4.9 %copy-start = (bf16[8,768]{1,0:T(8,128)(2,1)S(1)}, bf16[8,768]{1,0:T(8,128)(2,1)}, u32[]{:S(2)}) copy-start(bf16[8,768]{1,0:T(8,128)(2,1)} %own_ref.1) | copy-start | bytes 36868
  0.7 22.6 %copy-start.3 = (s32[16]{0:T(128)S(1)}, s32[16]{0:T(128)}, u32[]{:S(2)}) copy-start(s32[16]{0:T(128)} %param.9) | copy-start | bytes 196
  0.7 22.7 %copy-start.1 = (bf16[16,768]{1,0:T(8,128)(2,1)S(1)}, bf16[16,768]{1,0:T(8,128)(2,1)}, u32[]{:S(2)}) copy-start(bf16[16,768]{1,0:T(8,128)(2,1)} %param.8) | copy-start | bytes 73732
  6.6 43.6 %all-to-all-start = ((bf16[64,8,896]{2,1,0:T(8,128)(2,1)}), bf16[64,8,896]{2,1,0:T(8,128)(2,1)S(1)}, u32[]{:S(2)}, u32[]{:S(2)}) async-start(bf16[64,8,896]{2,1,0:T(8,128)(2,1)} %broadcast_in_dim.2), calls=%async_computation | async-start | bytes 1835008 | tf_op jit(solution)/shard_map/all_to_all | solution.py:97
  23.4 3.1 %collective-permute-start = (bf16[16,896]{1,0:T(8,128)(2,1)S(1)}, bf16[16,896]{1,0:T(8,128)(2,1)S(1)}, u32[]{:S(2)}, u32[]{:S(2)}) collective-permute-start(bf16[16,896]{1,0:T(8,128)(2,1)S(1)} %pad_maximum_fusion.10), channel_id=1, source_target_pairs={{0,64},{64,0},{128,192},{192,128},{256,320},{320,256},{384,448},{4... | collective-permute-start | bytes 86024 | tf_op jit(solution)/shard_map/ppermute | solution.py:103
  26.5 7.6 %collective-permute-start.1 = (bf16[32,896]{1,0:T(8,128)(2,1)S(1)}, bf16[32,896]{1,0:T(8,128)(2,1)S(1)}, u32[]{:S(2)}, u32[]{:S(2)}) collective-permute-start(bf16[32,896]{1,0:T(8,128)(2,1)S(1)} %pad_maximum_fusion.9), channel_id=1, source_target_pairs={{0,256},{64,320},{128,384},{192,448},{256,0},{320,64},{384,128},{4... | collective-permute-start | bytes 172040 | tf_op jit(solution)/shard_map/ppermute | solution.py:103
  34.1 6.7 %collective-permute-start.2 = (bf16[64,896]{1,0:T(8,128)(2,1)S(1)}, bf16[64,896]{1,0:T(8,128)(2,1)S(1)}, u32[]{:S(2)}, u32[]{:S(2)}) collective-permute-start(bf16[64,896]{1,0:T(8,128)(2,1)S(1)} %pad_maximum_fusion.8), channel_id=1, source_target_pairs={{0,128},{64,192},{128,0},{192,64},{256,384},{320,448},{384,256},{4... | collective-permute-start | bytes 344072 | tf_op jit(solution)/shard_map/ppermute | solution.py:103

commit v2 on v1

v2 whole, which is shorter than its diff:
```python
import functools
import math

import jax
import jax.numpy as jnp
from jax import lax
from jax.experimental import pallas as pl
from jax.experimental.pallas import tpu as pltpu
from jax.sharding import PartitionSpec as P

LANES = 128
SLOTS = 4
PACKED = 64
LOG2E = math.log2(math.e)
NT = (((1,), (1,)), ((), ()))


def with_digits(rows, numbers, digits):
    parts = jnp.stack([(numbers >> (8 * k)) & 255 for k in range(digits)], axis=1)
    tail = jnp.pad(parts.astype(rows.dtype), ((0, 0), (0, LANES - digits)))
    return jnp.concatenate([rows, tail], axis=1)


def split3(x):
    hi = x.astype(jnp.bfloat16)
    rest = x - hi.astype(jnp.float32)
    mid = rest.astype(jnp.bfloat16)
    low = (rest - mid.astype(jnp.float32)).astype(jnp.bfloat16)
    return hi, mid, low


def iota(shape, dim):
    return lax.broadcasted_iota(jnp.int32, shape, dim)


def as_row(digit_rows, digits):
    turned = digit_rows.astype(jnp.float32).T
    row = turned[0:1]
    for k in range(1, digits):
        row = row + turned[k:k + 1] * 256.0**k
    return row


def plan_positives(pos, first, rows, own, shards):
    count = pos.shape[1]
    local = pos - first
    owned = (local >= 0.0) & (local < rows)
    holder = jnp.floor((pos + 0.5) * (1.0 / rows))
    lane = iota((1, count), 1)
    rank = jnp.zeros((1, count), jnp.float32)
    for k in range(1, own):
        same = (pltpu.roll(holder, k, 1) == holder) & (lane % own >= k)
        rank = rank + jnp.where(same, 1.0, 0.0)
    order = jnp.where(owned, 1.0, 0.0)
    k = 1
    while k < count:
        order = order + jnp.where(lane >= k, pltpu.roll(order, k, 1), 0.0)
        k *= 2
    hit = owned & (order == iota((PACKED, 1), 0).astype(jnp.float32) + 1.0)
    column = jnp.sum(jnp.where(hit, local + 1.0, 0.0), axis=1, keepdims=True) - 1.0
    place = ((lane // own) * SLOTS).astype(jnp.float32) + rank
    place = jnp.sum(jnp.where(hit, place + 1.0, 0.0), axis=1, keepdims=True) - 1.0
    held = jnp.sum(
        jnp.where(holder == iota((shards, 1), 0).astype(jnp.float32), 1.0, 0.0), axis=1, keepdims=True
    )
    spill = (jnp.max(rank) >= SLOTS) | (jnp.max(held) > PACKED)
    return column, place, spill


def partial_kernel(chunk, own, first_ref, got_ref, new_ref, table_ref, out_ref, spill_ref, scores_ref):
    count, width = got_ref.shape
    depth = width - LANES
    rows = table_ref.shape[0]
    extra = new_ref.shape[0]
    to_log2 = LOG2E / math.sqrt(depth)
    queries = got_ref[:, :depth]
    pos = as_row(got_ref[:, depth:], 3)
    column, place, spill = plan_positives(pos, first_ref[0].astype(jnp.float32), rows, own, count // own)
    spill_ref[0] = spill.astype(jnp.int32)

    new_digits = new_ref[:, depth:]
    new_row = as_row(new_digits, 2)
    weight = jnp.where(iota((1, LANES), 1) == 0, 1.0, jnp.where(iota((1, LANES), 1) == 1, 256.0, 0.0))
    new_column = jnp.sum(new_digits.astype(jnp.float32) * weight, axis=1, keepdims=True)

    spans = [(start, chunk) for start in range(0, rows, chunk)] + [(rows, extra)]

    def block_of(start, size):
        return new_ref[:, :depth] if start == rows else table_ref[start:start + size, :]

    names = []
    top = jnp.full((count, LANES), -jnp.inf, jnp.float32)
    for start, size in spans:
        part = lax.dot_general(queries, block_of(start, size), NT, preferred_element_type=jnp.float32)
        if start == rows:
            name = new_row
        else:
            name = (iota((1, size), 1) + start).astype(jnp.float32)
            gone = jnp.max(jnp.where(new_column == name, 1.0, 0.0), axis=0, keepdims=True) > 0.0
            name = jnp.where(gone, -2.0, name)
            part = jnp.where(gone, -jnp.inf, part)
        names.append(name)
        scores_ref[:, start:start + size] = part
        for at in range(0, size, LANES):
            top = jnp.maximum(top, part[:, at:at + LANES])
    top = jnp.max(top, axis=1, keepdims=True) * to_log2

    total = jnp.zeros((count, LANES), jnp.float32)
    summed = jnp.zeros((count + PACKED, depth), jnp.float32)
    for (start, size), name in zip(spans, names):
        weights = jnp.exp2(scores_ref[:, start:start + size] * to_log2 - top)
        for at in range(0, size, LANES):
            total = total + weights[:, at:at + LANES]
        chosen = jnp.where(column == name, 1.0, 0.0)
        both = jnp.concatenate([weights.astype(jnp.bfloat16), chosen.astype(jnp.bfloat16)], axis=0)
        summed = summed + jnp.dot(both, block_of(start, size), preferred_element_type=jnp.float32)
    total = jnp.sum(total, axis=1, keepdims=True)
    out_ref[:, :depth] = (summed[:count] / total).astype(jnp.bfloat16)

    packed = summed[count:].astype(jnp.bfloat16)
    place_row = jnp.broadcast_to(place, (PACKED, LANES)).T[0:1]
    row = iota((count, 1), 0)
    slot = (row // own) * SLOTS + (row % own) // 2
    spread = jnp.where(slot.astype(jnp.float32) == place_row, 1.0, 0.0).astype(jnp.bfloat16)
    spread = jnp.dot(spread, packed, preferred_element_type=jnp.float32)
    half = depth // 2
    out_ref[:, depth:depth + half] = jnp.where(row % 2 == 0, spread[:, :half], spread[:, half:]).astype(jnp.bfloat16)

    hi, mid, low = split3(jnp.broadcast_to(top + jnp.log2(total), (count, LANES)))
    lane = iota((1, LANES), 1)
    zero = jnp.zeros((count, LANES), jnp.bfloat16)
    out_ref[:, depth + half:] = jnp.where(lane == 0, hi, jnp.where(lane == 1, mid, jnp.where(lane == 2, low, zero)))


def combine(got_ref, own_ref, positive, grad_ref, loss_ref):
    own, depth = own_ref.shape
    scale = 1.0 / math.sqrt(depth)
    logs = jnp.sum(got_ref[:, :, depth + depth // 2:].astype(jnp.float32), axis=2, keepdims=True)
    top = jnp.max(logs, axis=0, keepdims=True)
    share = jnp.exp2(logs - top)
    total = jnp.sum(share, axis=0)
    summed = jnp.sum(got_ref[:, :, :depth].astype(jnp.float32) * share, axis=0)
    grad_ref[...] = (summed / total - positive) * scale
    pos_score = jnp.sum(own_ref[...].astype(jnp.float32) * positive, axis=1, keepdims=True) * scale
    loss = (top[0] + jnp.log2(total)) * (1.0 / LOG2E) - pos_score
    loss_ref[...] = jnp.broadcast_to(loss, (own, LANES))


def slots_kernel(rows, pos_ref, got_ref, own_ref, grad_ref, loss_ref):
    own, depth = own_ref.shape
    half = depth // 2
    holders = [pos_ref[a] // rows for a in range(own)]
    positive = jnp.zeros((own, depth), jnp.float32)
    line = iota((own, 1), 0)
    for a in range(own):
        slot = 0
        for b in range(a):
            slot = slot + jnp.where(holders[b] == holders[a], 1, 0)
        block = got_ref[holders[a], :, depth:depth + half].astype(jnp.float32)
        left = jnp.sum(jnp.where(line == 2 * slot, block, 0.0), axis=0, keepdims=True)
        right = jnp.sum(jnp.where(line == 2 * slot + 1, block, 0.0), axis=0, keepdims=True)
        positive = jnp.where(line == a, jnp.concatenate([left, right], axis=1), positive)
    combine(got_ref, own_ref, positive, grad_ref, loss_ref)


def rows_kernel(got_ref, own_ref, positive_ref, grad_ref, loss_ref):
    combine(got_ref, own_ref, positive_ref[...], grad_ref, loss_ref)


def per_device(queries, positives, cache, fresh, slots):
    own, depth = queries.shape
    rows = cache.shape[0]
    shards = lax.axis_size("shard")
    groups = lax.axis_size("group")
    count = shards * own
    first = lax.axis_index("shard") * rows

    sent = with_digits(queries, positives, 3)
    got = lax.all_to_all(
        jnp.broadcast_to(sent[None], (shards,) + sent.shape), "shard", 0, 0
    ).reshape(count, depth + LANES)

    new = with_digits(fresh, slots - first, 2)
    for bit in (1, 4, 2):
        other = lax.ppermute(new, "group", [(i, i ^ bit) for i in range(groups)])
        new = jnp.concatenate([new, other], axis=0)

    vmem = pl.BlockSpec(memory_space=pltpu.VMEM)
    smem = pl.BlockSpec(memory_space=pltpu.SMEM)
    width = depth + depth // 2 + LANES
    part, spill = pl.pallas_call(
        functools.partial(partial_kernel, 512, own),
        out_shape=(
            jax.ShapeDtypeStruct((count, width), jnp.bfloat16),
            jax.ShapeDtypeStruct((1,), jnp.int32),
        ),
        in_specs=[smem, vmem, vmem, vmem],
        out_specs=(vmem, smem),
        scratch_shapes=[pltpu.VMEM((count, rows + new.shape[0]), jnp.float32)],
        compiler_params=pltpu.CompilerParams(vmem_limit_bytes=48 * 1024 * 1024),
        cost_estimate=pl.CostEstimate(
            flops=4 * count * rows * depth, bytes_accessed=2 * rows * depth, transcendentals=count * rows
        ),
    )(first.reshape(1).astype(jnp.int32), got, new, cache)

    back = lax.all_to_all(part.reshape(shards, own, width), "shard", 0, 0)
    outs = (
        jax.ShapeDtypeStruct((own, depth), jnp.float32),
        jax.ShapeDtypeStruct((own, LANES), jnp.float32),
    )
    params = pltpu.CompilerParams(vmem_limit_bytes=32 * 1024 * 1024)

    def from_slots():
        return pl.pallas_call(
            functools.partial(slots_kernel, rows), out_shape=outs,
            in_specs=[smem, vmem, vmem], out_specs=(vmem, vmem), compiler_params=params,
        )(positives, back, queries)

    def from_rows():
        digits = got[:, depth:depth + 3].astype(jnp.int32)
        local = digits[:, 0] + 256 * digits[:, 1] + 65536 * digits[:, 2] - first
        at = new[:, depth:depth + 2].astype(jnp.int32)
        is_new = local[:, None] == (at[:, 0] + 256 * at[:, 1])[None, :]
        new_rows = jnp.dot(
            is_new.astype(jnp.bfloat16), new[:, :depth], preferred_element_type=jnp.float32
        ).astype(jnp.bfloat16)
        old_rows = cache[jnp.clip(local, 0, rows - 1)]
        owned = (local >= 0) & (local < rows)
        picked = jnp.where(jnp.any(is_new, axis=1)[:, None], new_rows, jnp.where(owned[:, None], old_rows, 0))
        picked = lax.all_to_all(picked.reshape(shards, own, depth), "shard", 0, 0)
        positive = jnp.sum(picked.astype(jnp.float32), axis=0)
        return pl.pallas_call(
            rows_kernel, out_shape=outs,
            in_specs=[vmem, vmem, vmem], out_specs=(vmem, vmem), compiler_params=params,
        )(back, queries, positive)

    grad, loss = lax.cond(spill[0] > 0, from_rows, from_slots)
    return grad, loss[:, 0]


def solution(mesh):
    return jax.shard_map(
        per_device,
        mesh=mesh,
        in_specs=(
            P(("group", "shard"), None),
            P(("group", "shard")),
            P("shard", None),
            P(("group", "shard"), None),
            P(("group", "shard")),
        ),
        out_specs=(P(("group", "shard"), None), P(("group", "shard"))),
        check_vma=False,
    )
```

time: 116 us -> 102 us (0.88)
  blocking collectives: 52.4 us -> 0 us
  waiting for transfers between devices: 12.1 us -> 52.7 us
  starting transfers between devices: 24.5 us -> 30.8 us
  other arithmetic: 6.77 us -> 1.46 us
  local copies, waits for them, and re-layouts: 6.67 us -> 1.87 us
    all_to_all x1 -> x0, blocking collectives: 52.4 us -> none  [per_device(): back = lax.all_to_all(part.reshape(shards, own, width), 'shard', 0, 0)]
    all_to_all x0 -> x1, waiting for transfers between devices: none -> 33.9 us  [per_device(): back = lax.all_to_all(part.reshape(shards, own, width), 'shard', 0, 0)]
    all_to_all x1, waiting for transfers between devices: 2.76 us -> 9.45 us  [per_device(): lax.all_to_all(jnp.broadcast_to(sent[None], (shards,) + sent.shape), 'sha...]
    scatter x1 -> x0, other arithmetic: 6.52 us -> none  [per_device(): cache.at[at[:, 0] + 256 * at[:, 1]]]
    all_to_all x0 -> x1, starting transfers between devices: none -> 6.28 us  [per_device(): back = lax.all_to_all(part.reshape(shards, own, width), 'shard', 0, 0)]
    unnamed x11 -> x9, local copies, waits for them, and re-layouts: 4.99 us -> 0.12 us
  transfers between devices with their start and end apart: 4 -> 5, of which waited for: 4 -> 5; matrix products, arithmetic and copies ran while one was open for 6% -> 0% of each run, Pallas kernels for 0% -> 0%
where the time goes in v2:
time: 102 us; the launch traced here: 101 us
  waiting for transfers between devices  52.7 us (52%)
  starting transfers between devices  30.8 us (30%)
  Pallas kernels  12.8 us (13%)
  local copies, waits for them, and re-layouts  1.87 us (2%)
  other arithmetic  1.46 us (1%)
  between operations  1.4 us (1%)
    all_to_all x1, waiting for transfers between devices, per_device(): back = lax.all_to_all(part.reshape(shards, own, width), 'shard', 0, 0)  33.9 us
    all_to_all x1, starting transfers between devices, per_device(): lax.all_to_all(jnp.broadcast_to(sent[None], (shards,) + sent.shape), 'sha...  16.6 us
    pallas_call x1, Pallas kernels, per_device(): pl.pallas_call(functools.partial(partial_kernel, 512, own), out_shape=(ja...  11.2 us
    all_to_all x1, waiting for transfers between devices, per_device(): lax.all_to_all(jnp.broadcast_to(sent[None], (shards,) + sent.shape), 'sha...  9.45 us
    ppermute x3, waiting for transfers between devices, per_device(): other = lax.ppermute(new, 'group', [(i, i ^ bit) for i in range(groups)])  9.36 us
    ppermute x3, starting transfers between devices, per_device(): other = lax.ppermute(new, 'group', [(i, i ^ bit) for i in range(groups)])  7.96 us
    all_to_all x1, starting transfers between devices, per_device(): back = lax.all_to_all(part.reshape(shards, own, width), 'shard', 0, 0)  6.28 us
  transfers between devices with their start and end apart: 5, of which 5 were waited for; matrix products, arithmetic and copies ran while one was open for 0% of the time, Pallas kernels for 0%

profile of v2, /device:TPU:6, one launch (start us, length us, event | category | flops | bytes accessed | tf_op | source)
XLA Modules:
  0.0 101.1 jit_solution(118351119786932600)
XLA Ops:
  0.6 0.0 copy-start.5
  0.6 0.0 copy-start
  0.6 0.7 convert_bitcast_fusion.4
  1.3 0.1 copy.26
  1.4 0.7 fusion.10
  2.1 1.0 %broadcast_in_dim.33 = bf16[64,8,896]{2,1,0:T(8,128)(2,1)} broadcast(bf16[8,896]{1,0:T(8,128)(2,1)S(1)} %fusion.10), dimensions={1,2} | broadcast | bytes 931840 | tf_op jit(solution)/shard_map/broadcast_in_dim | solution.py:180
  3.2 16.6 %all-to-all-start.1 = ((bf16[64,8,896]{2,1,0:T(8,128)(2,1)}), bf16[64,8,896]{2,1,0:T(8,128)(2,1)S(1)}, u32[]{:S(2)}, u32[]{:S(2)}) async-start(bf16[64,8,896]{2,1,0:T(8,128)(2,1)} %broadcast_in_dim.33), calls=%async_computation.1 | async-start | bytes 1835008 | tf_op jit(solution)/shard_map/all_to_all | solution.py:179
  19.8 0.0 copy-done.5
  19.8 0.1 copy.23
  19.9 0.0 copy-done
  19.9 1.9 %collective-permute-start = (bf16[16,896]{1,0:T(8,128)(2,1)S(1)}, bf16[16,896]{1,0:T(8,128)(2,1)S(1)}, u32[]{:S(2)}, u32[]{:S(2)}) collective-permute-start(bf16[16,896]{1,0:T(8,128)(2,1)S(1)} %pad_maximum_fusion.3), channel_id=1, source_target_pairs={{0,64},{64,0},{128,192},{192,128},{256,320},{320,256},{384,448},{4... | collective-permute-start | bytes 86024 | tf_op jit(solution)/shard_map/ppermute | solution.py:185
  21.9 1.2 %collective-permute-done = bf16[16,896]{1,0:T(8,128)(2,1)S(1)} collective-permute-done((bf16[16,896]{1,0:T(8,128)(2,1)S(1)}, bf16[16,896]{1,0:T(8,128)(2,1)S(1)}, u32[]{:S(2)}, u32[]{:S(2)}) %collective-permute-start) | collective-permute-done | bytes 28704 | tf_op jit(solution)/shard_map/ppermute | solution.py:185
  23.0 3.3 %collective-permute-start.1 = (bf16[32,896]{1,0:T(8,128)(2,1)S(1)}, bf16[32,896]{1,0:T(8,128)(2,1)S(1)}, u32[]{:S(2)}, u32[]{:S(2)}) collective-permute-start(bf16[32,896]{1,0:T(8,128)(2,1)S(1)} %pad_maximum_fusion.2), channel_id=1, source_target_pairs={{0,256},{64,320},{128,384},{192,448},{256,0},{320,64},{384,128},{4... | collective-permute-start | bytes 172040 | tf_op jit(solution)/shard_map/ppermute | solution.py:185
  26.3 4.3 %collective-permute-done.1 = bf16[32,896]{1,0:T(8,128)(2,1)S(1)} collective-permute-done((bf16[32,896]{1,0:T(8,128)(2,1)S(1)}, bf16[32,896]{1,0:T(8,128)(2,1)S(1)}, u32[]{:S(2)}, u32[]{:S(2)}) %collective-permute-start.1) | collective-permute-done | bytes 57376 | tf_op jit(solution)/shard_map/ppermute | solution.py:185
  30.6 2.7 %collective-permute-start.2 = (bf16[64,896]{1,0:T(8,128)(2,1)S(1)}, bf16[64,896]{1,0:T(8,128)(2,1)S(1)}, u32[]{:S(2)}, u32[]{:S(2)}) collective-permute-start(bf16[64,896]{1,0:T(8,128)(2,1)S(1)} %pad_maximum_fusion.1), channel_id=1, source_target_pairs={{0,128},{64,192},{128,0},{192,64},{256,384},{320,448},{384,256},{4... | collective-permute-start | bytes 344072 | tf_op jit(solution)/shard_map/ppermute | solution.py:185
  33.4 3.9 %collective-permute-done.2 = bf16[64,896]{1,0:T(8,128)(2,1)S(1)} collective-permute-done((bf16[64,896]{1,0:T(8,128)(2,1)S(1)}, bf16[64,896]{1,0:T(8,128)(2,1)S(1)}, u32[]{:S(2)}, u32[]{:S(2)}) %collective-permute-start.2) | collective-permute-done | bytes 114720 | tf_op jit(solution)/shard_map/ppermute | solution.py:185
  37.3 9.4 %all-to-all-done.1 = bf16[64,8,896]{2,1,0:T(8,128)(2,1)S(1)} async-done(((bf16[64,8,896]{2,1,0:T(8,128)(2,1)}), bf16[64,8,896]{2,1,0:T(8,128)(2,1)S(1)}, u32[]{:S(2)}, u32[]{:S(2)}) %all-to-all-start.1) | async-done | bytes 917536 | tf_op jit(solution)/shard_map/all_to_all | solution.py:179
  46.8 11.2 %shard_map.70 = (bf16[512,1280]{1,0:T(8,128)(2,1)}, s32[1]{0:T(128)}) custom-call(s32[1]{0:T(128)} %bitcast.4.first_ref, bf16[512,896]{1,0:T(8,128)(2,1)S(1)} %bitcast.20, bf16[128,896]{1,0:T(8,128)(2,1)S(1)} %pad_maximum_fusion.new_ref, bf16[3072,768]{1,0:T(8,128)(2,1)} %table_ref.1), custom_call_target="tpu_custom_call" | custom-call | flops 4831838208 | bytes 4718592 | tf_op jit(solution)/shard_map/pallas_call | solution.py:191
  58.0 0.0 copy-start.3
  58.0 0.0 copy-start.4
  58.0 6.3 %all-to-all-start.2 = ((bf16[64,8,1280]{2,1,0:T(8,128)(2,1)}), bf16[64,8,1280]{2,1,0:T(8,128)(2,1)S(1)}, u32[]{:S(2)}, u32[]{:S(2)}) async-start(bf16[64,8,1280]{2,1,0:T(8,128)(2,1)} %bitcast.12), calls=%async_computation.2 | async-start | bytes 2621440 | tf_op jit(solution)/shard_map/all_to_all | solution.py:206
  65.0 33.9 %all-to-all-done.2 = bf16[64,8,1280]{2,1,0:T(8,128)(2,1)S(1)} async-done(((bf16[64,8,1280]{2,1,0:T(8,128)(2,1)}), bf16[64,8,1280]{2,1,0:T(8,128)(2,1)S(1)}, u32[]{:S(2)}, u32[]{:S(2)}) %all-to-all-start.2) | async-done | bytes 1310752 | tf_op jit(solution)/shard_map/all_to_all | solution.py:206
  98.9 0.0 copy-done.3
  98.9 0.0 copy-done.4
  98.9 2.2 %conditional.1 = (f32[8,768]{1,0:T(8,128)}, f32[8]{0:T(128)}) conditional(s32[]{:T(128)} %bitcast.11, (s32[8]{0:T(128)S(1)}, bf16[64,8,1280]{2,1,0:T(8,128)(2,1)S(1)}, bf16[8,768]{1,0:T(8,128)(2,1)S(1)}) %tuple.34, (bf16[512,896]{1,0:T(8,128)(2,1)S(1)}, s32[]{:T(128)}, bf16[128,896]{1,0:T(8,128)(2,1)S(1)}, bf16[3072,768]{1,0:T(8,128)(2,1)}, ...), branch_computations={%region_0.1_spmd, %region_1.4_spmd} | conditional | flops 102828544 | bytes 9895052 | solution.py:237
  98.9 1.5 %branch_0_fun.1 = (f32[8,768]{1,0:T(8,128)}, f32[8,128]{1,0:T(8,128)S(1)}) custom-call(s32[8]{0:T(128)S(1)} %get-tuple-element.23.pos_ref, bf16[64,8,1280]{2,1,0:T(8,128)(2,1)S(1)} %get-tuple-element.24.got_ref, bf16[8,768]{1,0:T(8,128)(2,1)S(1)} %get-tuple-element.25.own_ref), custom_call_target="tpu_custom_call" | custom-call | tf_op jit(solution)/shard_map/cond/branch_0_fun/pallas_call | solution.py:214
  100.4 0.6 slice_reduce_fusion
  (8 shorter events, 0.1 us)
Async XLA Ops:
  0.6 19.1 %copy-start.5 = (s32[16]{0:T(128)S(1)}, s32[16]{0:T(128)}, u32[]{:S(2)}) copy-start(s32[16]{0:T(128)} %param.11) | copy-start | bytes 196
  0.6 19.3 %copy-start = (bf16[16,768]{1,0:T(8,128)(2,1)S(1)}, bf16[16,768]{1,0:T(8,128)(2,1)}, u32[]{:S(2)}) copy-start(bf16[16,768]{1,0:T(8,128)(2,1)} %param.10) | copy-start | bytes 73732
  3.2 43.6 %all-to-all-start.1 = ((bf16[64,8,896]{2,1,0:T(8,128)(2,1)}), bf16[64,8,896]{2,1,0:T(8,128)(2,1)S(1)}, u32[]{:S(2)}, u32[]{:S(2)}) async-start(bf16[64,8,896]{2,1,0:T(8,128)(2,1)} %broadcast_in_dim.33), calls=%async_computation.1 | async-start | bytes 1835008 | tf_op jit(solution)/shard_map/all_to_all | solution.py:179
  19.9 3.1 %collective-permute-start = (bf16[16,896]{1,0:T(8,128)(2,1)S(1)}, bf16[16,896]{1,0:T(8,128)(2,1)S(1)}, u32[]{:S(2)}, u32[]{:S(2)}) collective-permute-start(bf16[16,896]{1,0:T(8,128)(2,1)S(1)} %pad_maximum_fusion.3), channel_id=1, source_target_pairs={{0,64},{64,0},{128,192},{192,128},{256,320},{320,256},{384,448},{4... | collective-permute-start | bytes 86024 | tf_op jit(solution)/shard_map/ppermute | solution.py:185
  23.0 7.6 %collective-permute-start.1 = (bf16[32,896]{1,0:T(8,128)(2,1)S(1)}, bf16[32,896]{1,0:T(8,128)(2,1)S(1)}, u32[]{:S(2)}, u32[]{:S(2)}) collective-permute-start(bf16[32,896]{1,0:T(8,128)(2,1)S(1)} %pad_maximum_fusion.2), channel_id=1, source_target_pairs={{0,256},{64,320},{128,384},{192,448},{256,0},{320,64},{384,128},{4... | collective-permute-start | bytes 172040 | tf_op jit(solution)/shard_map/ppermute | solution.py:185
  30.6 6.7 %collective-permute-start.2 = (bf16[64,896]{1,0:T(8,128)(2,1)S(1)}, bf16[64,896]{1,0:T(8,128)(2,1)S(1)}, u32[]{:S(2)}, u32[]{:S(2)}) collective-permute-start(bf16[64,896]{1,0:T(8,128)(2,1)S(1)} %pad_maximum_fusion.1), channel_id=1, source_target_pairs={{0,128},{64,192},{128,0},{192,64},{256,384},{320,448},{384,256},{4... | collective-permute-start | bytes 344072 | tf_op jit(solution)/shard_map/ppermute | solution.py:185
  58.0 40.9 %copy-start.3 = (bf16[8,768]{1,0:T(8,128)(2,1)S(1)}, bf16[8,768]{1,0:T(8,128)(2,1)}, u32[]{:S(2)}) copy-start(bf16[8,768]{1,0:T(8,128)(2,1)} %param.7) | copy-start | bytes 36868
  58.0 40.9 %copy-start.4 = (s32[8]{0:T(128)S(1)}, s32[8]{0:T(128)}, u32[]{:S(2)}) copy-start(s32[8]{0:T(128)} %param.8) | copy-start | bytes 100
  58.0 40.9 %all-to-all-start.2 = ((bf16[64,8,1280]{2,1,0:T(8,128)(2,1)}), bf16[64,8,1280]{2,1,0:T(8,128)(2,1)S(1)}, u32[]{:S(2)}, u32[]{:S(2)}) async-start(bf16[64,8,1280]{2,1,0:T(8,128)(2,1)} %bitcast.12), calls=%async_computation.2 | async-start | bytes 2621440 | tf_op jit(solution)/shard_map/all_to_all | solution.py:206

commit v3 on v2

v3 whole, which is shorter than its diff:
```python
import functools
import math

import jax
import jax.numpy as jnp
from jax import lax
from jax.experimental import pallas as pl
from jax.experimental.pallas import tpu as pltpu
from jax.sharding import PartitionSpec as P

LANES = 128
SIDE = 8
SLOTS = 12
TAIL = 16
CHUNK = 1024
PACKED = 64
LOG2E = math.log2(math.e)
NT = (((1,), (1,)), ((), ()))


def with_digits(rows, numbers, digits):
    parts = jnp.stack([(numbers >> (8 * k)) & 255 for k in range(digits)], axis=1)
    tail = jnp.pad(parts.astype(rows.dtype), ((0, 0), (0, LANES - digits)))
    return jnp.concatenate([rows, tail], axis=1)


def sent_kernel(digits, pos_ref, rows_ref, out_ref):
    own, depth = rows_ref.shape
    line, lane = iota((own, LANES), 0), iota((own, LANES), 1)
    tail = jnp.zeros((own, LANES), jnp.float32)
    for a in range(own):
        for k in range(digits):
            digit = ((pos_ref[a] >> (8 * k)) & 255).astype(jnp.float32)
            tail = jnp.where((line == a) & (lane == k), digit, tail)
    whole = jnp.concatenate([rows_ref[...], tail.astype(rows_ref.dtype)], axis=1)
    out_ref[...] = jnp.broadcast_to(whole[None], out_ref.shape)


def split3(x):
    hi = x.astype(jnp.bfloat16)
    rest = x - hi.astype(jnp.float32)
    mid = rest.astype(jnp.bfloat16)
    low = (rest - mid.astype(jnp.float32)).astype(jnp.bfloat16)
    return hi, mid, low


def iota(shape, dim):
    return lax.broadcasted_iota(jnp.int32, shape, dim)


def as_row(digit_rows, digits):
    turned = digit_rows.astype(jnp.float32).T
    row = turned[0:1]
    for k in range(1, digits):
        row = row + turned[k:k + 1] * 256.0**k
    return row


def plan_positives(pos, first, rows, shards, sides):
    count = pos.shape[1]
    local = pos - first
    owned = (local >= 0.0) & (local < rows)
    holder = jnp.floor((pos + 0.5) * (1.0 / rows))
    lane = iota((1, count), 1)
    block = lane // (count // sides)
    order = jnp.where(owned, 1.0, 0.0)
    k = 1
    while k < count:
        order = order + jnp.where(lane >= k, pltpu.roll(order, k, 1), 0.0)
        k *= 2
    before = jnp.zeros((1, count), jnp.float32)
    held = jnp.zeros((shards, 1), jnp.float32)
    most = 0.0
    is_holder = jnp.where(holder == iota((shards, 1), 0).astype(jnp.float32), 1.0, 0.0)
    for b in range(sides):
        here = block == b
        earlier = jnp.max(jnp.where(block < b, order, 0.0))
        before = jnp.where(here, earlier, before)
        part = jnp.sum(jnp.where(here, is_holder, 0.0), axis=1, keepdims=True)
        most = jnp.maximum(most, jnp.max(part))
        held = held + part
    spill = (most > SLOTS) | (jnp.max(held) > PACKED)
    slot = jnp.where(owned, order - before, 0.0)
    place = jnp.where(slot <= SLOTS, (block * TAIL).astype(jnp.float32) + slot, 0.0)
    hit = owned & (order == iota((PACKED, 1), 0).astype(jnp.float32) + 1.0)
    column = jnp.sum(jnp.where(hit, local + 1.0, 0.0), axis=1, keepdims=True) - 1.0
    place = jnp.sum(jnp.where(hit, place, 0.0), axis=1, keepdims=True) - 1.0
    return column, place, slot, spill


def partial_kernel(chunk, shards, first_ref, got_ref, new_ref, cache_ref, out_ref, spill_ref, table_ref, scores_ref, both_ref, sems):
    count, width = got_ref.shape
    depth = width - LANES
    rows = cache_ref.shape[0]
    extra = new_ref.shape[0]
    to_log2 = LOG2E / math.sqrt(depth)
    loads = []
    for start in range(0, rows, chunk):
        span = pl.ds(start, chunk)
        loads.append(pltpu.make_async_copy(cache_ref.at[span, :], table_ref.at[span, :], sems.at[start // chunk]))
        if len(loads) <= 2:
            loads[-1].start()
    pos = as_row(got_ref[:, depth:], 3)
    column, place, slot, spill = plan_positives(pos, first_ref[0].astype(jnp.float32), rows, shards, SIDE)
    spill_ref[0] = spill.astype(jnp.int32)

    new_digits = new_ref[:, depth:]
    new_row = as_row(new_digits, 2)
    weight = jnp.where(iota((1, LANES), 1) == 0, 1.0, jnp.where(iota((1, LANES), 1) == 1, 256.0, 0.0))
    new_column = jnp.sum(new_digits.astype(jnp.float32) * weight, axis=1, keepdims=True)

    spans = [(start, chunk) for start in range(0, rows, chunk)] + [(rows, extra)]

    def block_of(start, size):
        return new_ref[:, :depth] if start == rows else table_ref[start:start + size, :]

    names, dead = [], []
    for start, size in spans:
        name, gone = new_row, None
        if start < rows:
            name = (iota((1, size), 1) + start).astype(jnp.float32)
            gone = jnp.max(jnp.where(new_column == name, 1.0, 0.0), axis=0, keepdims=True) > 0.0
            name = jnp.where(gone, -2.0, name)
        names.append(name)
        dead.append(gone)
    for (start, size), name in zip(spans, names):
        both_ref[count:, start:start + size] = jnp.where(column == name, 1.0, 0.0).astype(jnp.bfloat16)

    part_count = count // 2
    tops, totals = [], []
    for at_row in (0, part_count):
        mine = slice(at_row, at_row + part_count)
        top = jnp.full((part_count, LANES), -jnp.inf, jnp.float32)
        for (start, size), gone in zip(spans, dead):
            if at_row == 0 and start < rows:
                loads[start // chunk].wait()
                if start // chunk + 2 < len(loads):
                    loads[start // chunk + 2].start()
            part = lax.dot_general(
                got_ref[mine, :depth], block_of(start, size), NT, preferred_element_type=jnp.float32
            )
            if gone is not None:
                part = jnp.where(gone, -jnp.inf, part)
            scores_ref[mine, start:start + size] = part
            for at in range(0, size, LANES):
                top = jnp.maximum(top, part[:, at:at + LANES])
        top = jnp.max(top, axis=1, keepdims=True) * to_log2
        total = jnp.zeros((part_count, LANES), jnp.float32)
        for start, size in spans:
            weights = jnp.exp2(scores_ref[mine, start:start + size] * to_log2 - top)
            for at in range(0, size, LANES):
                total = total + weights[:, at:at + LANES]
            both_ref[mine, start:start + size] = weights.astype(jnp.bfloat16)
        tops.append(top)
        totals.append(total)
    top, total = jnp.concatenate(tops, axis=0), jnp.concatenate(totals, axis=0)
    sums = []
    for mine in (slice(0, part_count), slice(part_count, count + PACKED)):
        part = jnp.dot(both_ref[mine, :rows], table_ref[...], preferred_element_type=jnp.float32)
        sums.append(part + jnp.dot(both_ref[mine, rows:], new_ref[:, :depth], preferred_element_type=jnp.float32))
    summed = jnp.concatenate(sums, axis=0)
    total = jnp.sum(total, axis=1, keepdims=True)
    mean = (summed[:count] / total).astype(jnp.bfloat16)

    packed = summed[count:].astype(jnp.bfloat16)
    place_row = jnp.broadcast_to(place, (PACKED, LANES)).T[0:1]
    spread = jnp.where(iota((SIDE * TAIL, 1), 0).astype(jnp.float32) == place_row, 1.0, 0.0).astype(jnp.bfloat16)
    spread = jnp.dot(spread, packed, preferred_element_type=jnp.float32)
    logs = jnp.broadcast_to(top + jnp.log2(total), (count, LANES)).T[0:1]
    facts = [part.astype(jnp.float32) for part in split3(logs)] + [slot]
    block = count // SIDE
    line, lane = iota((TAIL, LANES), 0), iota((TAIL, LANES), 1)
    for b in range(SIDE):
        at = b * block // LANES * LANES
        tail = spread[b * TAIL:(b + 1) * TAIL]
        first_tile = tail[:, :LANES]
        for k, fact in enumerate(facts):
            piece = fact[:, at:at + LANES]
            if b * block % LANES:
                piece = pltpu.roll(piece, LANES - b * block % LANES, 1)
            first_tile = jnp.where((line == SLOTS + k) & (lane < block), piece, first_tile)
        out_ref[b, :block, :] = mean[b * block:(b + 1) * block]
        out_ref[b, block:, :LANES] = first_tile.astype(jnp.bfloat16)
        out_ref[b, block:, LANES:] = tail[:, LANES:].astype(jnp.bfloat16)


def block_kernel(got_ref, out_ref):
    sources, lines, depth = got_ref.shape
    block = lines - TAIL
    source = iota((sources, LANES), 0)
    logs = jnp.zeros((sources, LANES), jnp.float32)
    slot = jnp.zeros((sources, LANES), jnp.float32)
    for s in range(sources):
        tail = got_ref[s, block:, :LANES].astype(jnp.float32)
        log = tail[SLOTS:SLOTS + 1] + tail[SLOTS + 1:SLOTS + 2] + tail[SLOTS + 2:SLOTS + 3]
        logs = jnp.where(source == s, log, logs)
        slot = jnp.where(source == s, tail[SLOTS + 3:SLOTS + 4], slot)
    top = jnp.max(logs, axis=0, keepdims=True)
    share = jnp.exp2(logs - top)
    total = jnp.sum(share, axis=0, keepdims=True)
    share = share / total
    whole = jnp.broadcast_to(top + jnp.log2(total), (sources, LANES))
    rest = jnp.zeros((LANES - 3 * sources, LANES), jnp.float32)
    turned = jnp.concatenate([share, slot, whole, rest], axis=0).T[:block]

    summed = jnp.zeros((block, depth), jnp.float32)
    for s in range(sources):
        summed = summed + got_ref[s, :block, :].astype(jnp.float32) * turned[:, s:s + 1]
    lane = iota((1, sources * TAIL), 1)
    wanted = jnp.zeros((block, sources * TAIL), jnp.float32)
    for s in range(sources):
        wanted = jnp.where(lane // TAIL == s, turned[:, sources + s:sources + s + 1], wanted)
    chosen = jnp.where(wanted == (lane % TAIL + 1).astype(jnp.float32), 1.0, 0.0).astype(jnp.bfloat16)
    slots = jnp.concatenate([got_ref[s, block:, :] for s in range(sources)], axis=0)
    positive = jnp.dot(chosen, slots, preferred_element_type=jnp.float32)
    out_ref[:, :depth] = summed.astype(jnp.bfloat16)
    out_ref[:, depth:2 * depth] = positive.astype(jnp.bfloat16)
    hi, mid, low = split3(jnp.broadcast_to(turned[:, 2 * sources:2 * sources + 1], (block, LANES)))
    lane = iota((1, LANES), 1)
    zero = jnp.zeros((block, LANES), jnp.bfloat16)
    out_ref[:, 2 * depth:] = jnp.where(lane == 0, hi, jnp.where(lane == 1, mid, jnp.where(lane == 2, low, zero)))


def combine(got_ref, own_ref, positive, grad_ref, loss_ref):
    own, depth = own_ref.shape
    scale = 1.0 / math.sqrt(depth)
    logs = jnp.sum(got_ref[:, :, 2 * depth:].astype(jnp.float32), axis=2, keepdims=True)
    top = jnp.max(logs, axis=0, keepdims=True)
    share = jnp.exp2(logs - top)
    total = jnp.sum(share, axis=0)
    summed = jnp.sum(got_ref[:, :, :depth].astype(jnp.float32) * share, axis=0)
    grad_ref[...] = (summed / total - positive) * scale
    pos_score = jnp.sum(own_ref[...].astype(jnp.float32) * positive, axis=1, keepdims=True) * scale
    loss = (top[0] + jnp.log2(total)) * (1.0 / LOG2E) - pos_score
    line, lane = iota((own, LANES), 0), iota((own, LANES), 1)
    loss_ref[...] = jnp.sum(jnp.where(line == lane, loss, 0.0), axis=0, keepdims=True)


def slots_kernel(got_ref, own_ref, grad_ref, loss_ref):
    depth = own_ref.shape[1]
    positive = jnp.sum(got_ref[:, :, depth:2 * depth].astype(jnp.float32), axis=0)
    combine(got_ref, own_ref, positive, grad_ref, loss_ref)


def rows_kernel(got_ref, own_ref, positive_ref, grad_ref, loss_ref):
    combine(got_ref, own_ref, positive_ref[...], grad_ref, loss_ref)


def routes(groups):
    plane, first_ring, second_ring = [], [], []
    for g in range(groups):
        table = [[g * SIDE * SIDE + z * SIDE + y for y in range(SIDE)] for z in range(SIDE)]
        turned = [list(column) for column in zip(*table)]
        if g % 2:
            table, turned = turned, table
        plane.append([device for row in table for device in row])
        first_ring += turned
        second_ring += table
    return plane, first_ring, second_ring


def per_device(queries, positives, cache, fresh, slots):
    own, depth = queries.shape
    rows = cache.shape[0]
    shards = lax.axis_size("shard")
    groups = lax.axis_size("group")
    count = shards * own
    every = ("group", "shard")
    plane, first_ring, second_ring = routes(groups)
    first = lax.axis_index("shard") * rows

    vmem = pl.BlockSpec(memory_space=pltpu.VMEM)
    smem = pl.BlockSpec(memory_space=pltpu.SMEM)
    sent = pl.pallas_call(
        functools.partial(sent_kernel, 3),
        out_shape=pltpu.VMEM((shards, own, depth + LANES), jnp.bfloat16),
        in_specs=[smem, vmem], out_specs=vmem,
    )(positives, queries)
    got = lax.all_to_all(sent, every, 0, 0, axis_index_groups=plane).reshape(count, depth + LANES)

    new = with_digits(fresh, slots - first, 2)
    for bit in (1, 4, 2):
        other = lax.ppermute(new, "group", [(i, i ^ bit) for i in range(groups)])
        new = jnp.concatenate([new, other], axis=0)

    block = count // SIDE
    width = 2 * depth + LANES
    part, spill = pl.pallas_call(
        functools.partial(partial_kernel, CHUNK, shards),
        out_shape=(
            pltpu.VMEM((SIDE, block + TAIL, depth), jnp.bfloat16),
            jax.ShapeDtypeStruct((1,), jnp.int32),
        ),
        in_specs=[smem, vmem, vmem, pl.BlockSpec(memory_space=pl.ANY)],
        out_specs=(vmem, smem),
        scratch_shapes=[
            pltpu.VMEM((rows, depth), jnp.bfloat16),
            pltpu.VMEM((count, rows + new.shape[0]), jnp.float32),
            pltpu.VMEM((count + PACKED, rows + new.shape[0]), jnp.bfloat16),
            pltpu.SemaphoreType.DMA((rows // CHUNK,)),
        ],
        compiler_params=pltpu.CompilerParams(vmem_limit_bytes=48 * 1024 * 1024),
        cost_estimate=pl.CostEstimate(
            flops=4 * count * rows * depth, bytes_accessed=2 * rows * depth, transcendentals=count * rows
        ),
    )(first.reshape(1).astype(jnp.int32), got, new, cache)

    part = lax.all_to_all(part, every, 0, 0, axis_index_groups=first_ring)
    part = pl.pallas_call(
        block_kernel,
        out_shape=pltpu.VMEM((block, width), jnp.bfloat16),
        in_specs=[vmem], out_specs=vmem,
        compiler_params=pltpu.CompilerParams(vmem_limit_bytes=32 * 1024 * 1024),
    )(part)
    back = lax.all_to_all(part.reshape(SIDE, own, width), every, 0, 0, axis_index_groups=second_ring)
    outs = (
        jax.ShapeDtypeStruct((own, depth), jnp.float32),
        jax.ShapeDtypeStruct((1, LANES), jnp.float32),
    )
    params = pltpu.CompilerParams(vmem_limit_bytes=32 * 1024 * 1024)

    def from_slots():
        return pl.pallas_call(
            slots_kernel, out_shape=outs,
            in_specs=[vmem, vmem], out_specs=(vmem, vmem), compiler_params=params,
        )(back, queries)

    def from_rows():
        digits = got[:, depth:depth + 3].astype(jnp.int32)
        local = digits[:, 0] + 256 * digits[:, 1] + 65536 * digits[:, 2] - first
        at = new[:, depth:depth + 2].astype(jnp.int32)
        is_new = local[:, None] == (at[:, 0] + 256 * at[:, 1])[None, :]
        new_rows = jnp.dot(
            is_new.astype(jnp.bfloat16), new[:, :depth], preferred_element_type=jnp.float32
        ).astype(jnp.bfloat16)
        old_rows = cache[jnp.clip(local, 0, rows - 1)]
        owned = (local >= 0) & (local < rows)
        picked = jnp.where(jnp.any(is_new, axis=1)[:, None], new_rows, jnp.where(owned[:, None], old_rows, 0))
        picked = lax.all_to_all(picked.reshape(shards, own, depth), every, 0, 0, axis_index_groups=plane)
        positive = jnp.sum(picked.astype(jnp.float32), axis=0)
        return pl.pallas_call(
            rows_kernel, out_shape=outs,
            in_specs=[vmem, vmem, vmem], out_specs=(vmem, vmem), compiler_params=params,
        )(back, queries, positive)

    grad, loss = lax.cond(spill[0] > 0, from_rows, from_slots)
    return grad, loss[0, :own]


def solution(mesh):
    return jax.shard_map(
        per_device,
        mesh=mesh,
        in_specs=(
            P(("group", "shard"), None),
            P(("group", "shard")),
            P("shard", None),
            P(("group", "shard"), None),
            P(("group", "shard")),
        ),
        out_specs=(P(("group", "shard"), None), P(("group", "shard"))),
        check_vma=False,
    )
```

time: 102 us -> 94.7 us (0.928)
  waiting for transfers between devices: 52.7 us -> 24.1 us
  blocking collectives: 0 us -> 22.7 us
  starting transfers between devices: 30.8 us -> 28 us
  other arithmetic: 1.46 us -> 3.67 us
  local copies, waits for them, and re-layouts: 1.87 us -> 0.62 us
    all_to_all x2, waiting for transfers between devices: 43.4 us -> 14.8 us  [the longest x1 9.3 us: per_device(): lax.all_to_all(part.reshape(SIDE, own, width), every, 0, 0, axis_index_gr...]
    all_to_all x0 -> x1, blocking collectives: none -> 22.7 us  [per_device(): part = lax.all_to_all(part, every, 0, 0, axis_index_groups=first_ring)]
    all_to_all x2, starting transfers between devices: 22.9 us -> 20.1 us  [the longest x1 16.6 us: per_device(): lax.all_to_all(sent, every, 0, 0, axis_index_groups=plane)]
    concatenate x3, other arithmetic: 0.04 us -> 2.25 us  [per_device(): new = jnp.concatenate([new, other], axis=0)]
    broadcast_in_dim x1 -> x0, local copies, waits for them, and re-layouts: 1.02 us -> none  [per_device(): jnp.broadcast_to(sent[None], (shards,) + sent.shape)]
    pallas_call x2 -> x4, Pallas kernels: 12.8 us -> 13.5 us  [the longest x1 9.78 us: per_device(): pl.pallas_call(functools.partial(partial_kernel, CHUNK, shards), out_shap...]
  transfers between devices with their start and end apart: 5 -> 5, of which waited for: 5 -> 5; matrix products, arithmetic and copies ran while one was open for 0% -> 4% of each run, Pallas kernels for 0% -> 0%
where the time goes in v3:
time: 94.7 us; the launch traced here: 93.9 us
  starting transfers between devices  28 us (30%)
  waiting for transfers between devices  24.1 us (25%)
  blocking collectives  22.7 us (24%)
  Pallas kernels  13.5 us (14%)
  other arithmetic  3.67 us (4%)
  between operations  1.34 us (1%)
    all_to_all x1, blocking collectives, per_device(): part = lax.all_to_all(part, every, 0, 0, axis_index_groups=first_ring)  22.7 us
    all_to_all x1, starting transfers between devices, per_device(): lax.all_to_all(sent, every, 0, 0, axis_index_groups=plane)  16.6 us
    pallas_call x1, Pallas kernels, per_device(): pl.pallas_call(functools.partial(partial_kernel, CHUNK, shards), out_shap...  9.78 us
    ppermute x3, waiting for transfers between devices, per_device(): other = lax.ppermute(new, 'group', [(i, i ^ bit) for i in range(groups)])  9.36 us
    all_to_all x1, waiting for transfers between devices, per_device(): lax.all_to_all(part.reshape(SIDE, own, width), every, 0, 0, axis_index_gr...  9.3 us
    ppermute x3, starting transfers between devices, per_device(): other = lax.ppermute(new, 'group', [(i, i ^ bit) for i in range(groups)])  7.95 us
    all_to_all x1, waiting for transfers between devices, per_device(): lax.all_to_all(sent, every, 0, 0, axis_index_groups=plane)  5.48 us
    all_to_all x1, starting transfers between devices, per_device(): lax.all_to_all(part.reshape(SIDE, own, width), every, 0, 0, axis_index_gr...  3.49 us
  transfers between devices with their start and end apart: 5, of which 5 were waited for; matrix products, arithmetic and copies ran while one was open for 4% of the time, Pallas kernels for 0%

profile of v3, /device:TPU:6, one launch (start us, length us, event | category | flops | bytes accessed | tf_op | source)
XLA Modules:
  0.0 93.9 jit_solution(10808685327890875693)
XLA Ops:
  0.6 1.7 %shard_map.70 = bf16[64,8,896]{2,1,0:T(8,128)(2,1)} custom-call(s32[8]{0:T(128)} %pos_ref.1, bf16[8,768]{1,0:T(8,128)(2,1)} %rows_ref.1), custom_call_target="tpu_custom_call" | custom-call | tf_op jit(solution)/shard_map/pallas_call | solution.py:274
  2.4 16.6 %all-to-all-start.1 = ((bf16[64,8,896]{2,1,0:T(8,128)(2,1)}), bf16[64,8,896]{2,1,0:T(8,128)(2,1)S(1)}, u32[]{:S(2)}, u32[]{:S(2)}) async-start(bf16[64,8,896]{2,1,0:T(8,128)(2,1)} %shard_map.70), calls=%async_computation.1 | async-start | bytes 1835008 | tf_op jit(solution)/shard_map/all_to_all | solution.py:279
  19.0 0.7 convert_bitcast_fusion.1
  19.6 0.1 copy.19
  19.8 0.7 pad_maximum_fusion.3
  20.5 1.9 %collective-permute-start = (bf16[16,896]{1,0:T(8,128)(2,1)S(1)}, bf16[16,896]{1,0:T(8,128)(2,1)S(1)}, u32[]{:S(2)}, u32[]{:S(2)}) collective-permute-start(bf16[16,896]{1,0:T(8,128)(2,1)S(1)} %pad_maximum_fusion.3), channel_id=1, source_target_pairs={{0,64},{64,0},{128,192},{192,128},{256,320},{320,256},{384,448},{4... | collective-permute-start | bytes 86024 | tf_op jit(solution)/shard_map/ppermute | solution.py:283
  22.4 1.2 %collective-permute-done = bf16[16,896]{1,0:T(8,128)(2,1)S(1)} collective-permute-done((bf16[16,896]{1,0:T(8,128)(2,1)S(1)}, bf16[16,896]{1,0:T(8,128)(2,1)S(1)}, u32[]{:S(2)}, u32[]{:S(2)}) %collective-permute-start) | collective-permute-done | bytes 28704 | tf_op jit(solution)/shard_map/ppermute | solution.py:283
  23.6 0.7 pad_maximum_fusion.2
  24.3 3.3 %collective-permute-start.1 = (bf16[32,896]{1,0:T(8,128)(2,1)S(1)}, bf16[32,896]{1,0:T(8,128)(2,1)S(1)}, u32[]{:S(2)}, u32[]{:S(2)}) collective-permute-start(bf16[32,896]{1,0:T(8,128)(2,1)S(1)} %pad_maximum_fusion.2), channel_id=1, source_target_pairs={{0,256},{64,320},{128,384},{192,448},{256,0},{320,64},{384,128},{4... | collective-permute-start | bytes 172040 | tf_op jit(solution)/shard_map/ppermute | solution.py:283
  27.6 4.3 %collective-permute-done.1 = bf16[32,896]{1,0:T(8,128)(2,1)S(1)} collective-permute-done((bf16[32,896]{1,0:T(8,128)(2,1)S(1)}, bf16[32,896]{1,0:T(8,128)(2,1)S(1)}, u32[]{:S(2)}, u32[]{:S(2)}) %collective-permute-start.1) | collective-permute-done | bytes 57376 | tf_op jit(solution)/shard_map/ppermute | solution.py:283
  31.9 0.7 pad_maximum_fusion.1
  32.6 2.7 %collective-permute-start.2 = (bf16[64,896]{1,0:T(8,128)(2,1)S(1)}, bf16[64,896]{1,0:T(8,128)(2,1)S(1)}, u32[]{:S(2)}, u32[]{:S(2)}) collective-permute-start(bf16[64,896]{1,0:T(8,128)(2,1)S(1)} %pad_maximum_fusion.1), channel_id=1, source_target_pairs={{0,128},{64,192},{128,0},{192,64},{256,384},{320,448},{384,256},{4... | collective-permute-start | bytes 344072 | tf_op jit(solution)/shard_map/ppermute | solution.py:283
  35.4 3.9 %collective-permute-done.2 = bf16[64,896]{1,0:T(8,128)(2,1)S(1)} collective-permute-done((bf16[64,896]{1,0:T(8,128)(2,1)S(1)}, bf16[64,896]{1,0:T(8,128)(2,1)S(1)}, u32[]{:S(2)}, u32[]{:S(2)}) %collective-permute-start.2) | collective-permute-done | bytes 114720 | tf_op jit(solution)/shard_map/ppermute | solution.py:283
  39.3 0.8 pad_maximum_fusion.new_ref
  40.1 5.5 %all-to-all-done.1 = bf16[64,8,896]{2,1,0:T(8,128)(2,1)S(1)} async-done(((bf16[64,8,896]{2,1,0:T(8,128)(2,1)}), bf16[64,8,896]{2,1,0:T(8,128)(2,1)S(1)}, u32[]{:S(2)}, u32[]{:S(2)}) %all-to-all-start.1) | async-done | bytes 917536 | tf_op jit(solution)/shard_map/all_to_all | solution.py:279
  45.6 0.0 copy-start
  45.6 9.8 %shard_map.71 = (bf16[8,80,768]{2,1,0:T(8,128)(2,1)S(1)}, s32[1]{0:T(128)}) custom-call(s32[1]{0:T(128)} %bitcast.6.first_ref, bf16[512,896]{1,0:T(8,128)(2,1)S(1)} %bitcast.18, bf16[128,896]{1,0:T(8,128)(2,1)S(1)} %pad_maximum_fusion.new_ref, bf16[3072,768]{1,0:T(8,128)(2,1)} %cache_ref.1), custom_call_target="tpu_custom_call" | custom-call | flops 4831838208 | bytes 4718592 | tf_op jit(solution)/shard_map/pallas_call | solution.py:288
  55.4 22.7 %all_to_all.20.got_ref = bf16[8,80,768]{2,1,0:T(8,128)(2,1)S(1)} all-to-all(bf16[8,80,768]{2,1,0:T(8,128)(2,1)S(1)} %get-tuple-element.38), channel_id=1, replica_groups={{0,8,16,24,32,40,48,56},{1,9,17,25,33,41,49,57},{2,10,18,26,34,42,50,58..., dimensions={0} | all-to-all | bytes 1966080 | tf_op jit(solution)/shard_map/all_to_all | solution.py:308
  78.0 1.2 %shard_map.72 = bf16[64,1664]{1,0:T(8,128)(2,1)} custom-call(bf16[8,80,768]{2,1,0:T(8,128)(2,1)S(1)} %all_to_all.20.got_ref), custom_call_target="tpu_custom_call" | custom-call | tf_op jit(solution)/shard_map/pallas_call | solution.py:309
  79.2 3.5 %all-to-all-start.3 = ((bf16[8,8,1664]{2,1,0:T(8,128)(2,1)}), bf16[8,8,1664]{2,1,0:T(8,128)(2,1)S(1)}, u32[]{:S(2)}, u32[]{:S(2)}) async-start(bf16[8,8,1664]{2,1,0:T(8,128)(2,1)} %bitcast.11), calls=%async_computation.3 | async-start | bytes 425984 | tf_op jit(solution)/shard_map/all_to_all | solution.py:315
  83.4 9.3 %all-to-all-done.3 = bf16[8,8,1664]{2,1,0:T(8,128)(2,1)S(1)} async-done(((bf16[8,8,1664]{2,1,0:T(8,128)(2,1)}), bf16[8,8,1664]{2,1,0:T(8,128)(2,1)S(1)}, u32[]{:S(2)}, u32[]{:S(2)}) %all-to-all-start.3) | async-done | bytes 213024 | tf_op jit(solution)/shard_map/all_to_all | solution.py:315
  92.7 0.0 copy-done
  92.7 1.2 %conditional.1 = (f32[8,768]{1,0:T(8,128)}, f32[8]{0:T(128)}) conditional(s32[]{:T(128)} %bitcast.10, (bf16[8,8,1664]{2,1,0:T(8,128)(2,1)S(1)}, bf16[8,768]{1,0:T(8,128)(2,1)S(1)}) %tuple.30, (bf16[512,896]{1,0:T(8,128)(2,1)S(1)}, s32[]{:T(128)}, bf16[128,896]{1,0:T(8,128)(2,1)S(1)}, bf16[3072,768]{1,0:T(8,128)(2,1)}, ...), branch_computations={%region_0.1_spmd, %region_1.4_spmd} | conditional | flops 102828544 | bytes 8059988 | solution.py:346
  92.7 0.7 branch_0_fun.1
  93.4 0.5 slice_bitcast_fusion
  (2 shorter events, 0.0 us)
Async XLA Ops:
  2.4 43.2 %all-to-all-start.1 = ((bf16[64,8,896]{2,1,0:T(8,128)(2,1)}), bf16[64,8,896]{2,1,0:T(8,128)(2,1)S(1)}, u32[]{:S(2)}, u32[]{:S(2)}) async-start(bf16[64,8,896]{2,1,0:T(8,128)(2,1)} %shard_map.70), calls=%async_computation.1 | async-start | bytes 1835008 | tf_op jit(solution)/shard_map/all_to_all | solution.py:279
  20.5 3.1 %collective-permute-start = (bf16[16,896]{1,0:T(8,128)(2,1)S(1)}, bf16[16,896]{1,0:T(8,128)(2,1)S(1)}, u32[]{:S(2)}, u32[]{:S(2)}) collective-permute-start(bf16[16,896]{1,0:T(8,128)(2,1)S(1)} %pad_maximum_fusion.3), channel_id=1, source_target_pairs={{0,64},{64,0},{128,192},{192,128},{256,320},{320,256},{384,448},{4... | collective-permute-start | bytes 86024 | tf_op jit(solution)/shard_map/ppermute | solution.py:283
  24.3 7.6 %collective-permute-start.1 = (bf16[32,896]{1,0:T(8,128)(2,1)S(1)}, bf16[32,896]{1,0:T(8,128)(2,1)S(1)}, u32[]{:S(2)}, u32[]{:S(2)}) collective-permute-start(bf16[32,896]{1,0:T(8,128)(2,1)S(1)} %pad_maximum_fusion.2), channel_id=1, source_target_pairs={{0,256},{64,320},{128,384},{192,448},{256,0},{320,64},{384,128},{4... | collective-permute-start | bytes 172040 | tf_op jit(solution)/shard_map/ppermute | solution.py:283
  32.6 6.7 %collective-permute-start.2 = (bf16[64,896]{1,0:T(8,128)(2,1)S(1)}, bf16[64,896]{1,0:T(8,128)(2,1)S(1)}, u32[]{:S(2)}, u32[]{:S(2)}) collective-permute-start(bf16[64,896]{1,0:T(8,128)(2,1)S(1)} %pad_maximum_fusion.1), channel_id=1, source_target_pairs={{0,128},{64,192},{128,0},{192,64},{256,384},{320,448},{384,256},{4... | collective-permute-start | bytes 344072 | tf_op jit(solution)/shard_map/ppermute | solution.py:283
  45.6 47.1 %copy-start = (bf16[8,768]{1,0:T(8,128)(2,1)S(1)}, bf16[8,768]{1,0:T(8,128)(2,1)}, u32[]{:S(2)}) copy-start(bf16[8,768]{1,0:T(8,128)(2,1)} %rows_ref.1) | copy-start | bytes 36868
  79.2 13.5 %all-to-all-start.3 = ((bf16[8,8,1664]{2,1,0:T(8,128)(2,1)}), bf16[8,8,1664]{2,1,0:T(8,128)(2,1)S(1)}, u32[]{:S(2)}, u32[]{:S(2)}) async-start(bf16[8,8,1664]{2,1,0:T(8,128)(2,1)} %bitcast.11), calls=%async_computation.3 | async-start | bytes 425984 | tf_op jit(solution)/shard_map/all_to_all | solution.py:315

commit v4 on v3

--- a/solution.py
+++ b/solution.py
@@ -18,22 +18,21 @@
 NT = (((1,), (1,)), ((), ()))
 
 
-def with_digits(rows, numbers, digits):
-    parts = jnp.stack([(numbers >> (8 * k)) & 255 for k in range(digits)], axis=1)
-    tail = jnp.pad(parts.astype(rows.dtype), ((0, 0), (0, LANES - digits)))
-    return jnp.concatenate([rows, tail], axis=1)
-
-
-def sent_kernel(digits, pos_ref, rows_ref, out_ref):
-    own, depth = rows_ref.shape
-    line, lane = iota((own, LANES), 0), iota((own, LANES), 1)
-    tail = jnp.zeros((own, LANES), jnp.float32)
-    for a in range(own):
+def with_digits(numbers, rows, digits):
+    line, lane = iota((len(numbers), LANES), 0), iota((len(numbers), LANES), 1)
+    tail = jnp.zeros((len(numbers), LANES), jnp.float32)
+    for n, number in enumerate(numbers):
         for k in range(digits):
-            digit = ((pos_ref[a] >> (8 * k)) & 255).astype(jnp.float32)
-            tail = jnp.where((line == a) & (lane == k), digit, tail)
-    whole = jnp.concatenate([rows_ref[...], tail.astype(rows_ref.dtype)], axis=1)
+            digit = ((number >> (8 * k)) & 255).astype(jnp.float32)
+            tail = jnp.where((line == n) & (lane == k), digit, tail)
+    return jnp.concatenate([rows, tail.astype(rows.dtype)], axis=1)
+
+
+def sent_kernel(first_ref, pos_ref, slots_ref, queries_ref, fresh_ref, out_ref, new_ref):
+    own, added = queries_ref.shape[0], fresh_ref.shape[0]
+    whole = with_digits([pos_ref[n] for n in range(own)], queries_ref[...], 3)
     out_ref[...] = jnp.broadcast_to(whole[None], out_ref.shape)
+    new_ref[...] = with_digits([slots_ref[n] - first_ref[0] for n in range(added)], fresh_ref[...], 2)
 
 
 def split3(x):
@@ -88,18 +87,18 @@
     return column, place, slot, spill
 
 
-def partial_kernel(chunk, shards, first_ref, got_ref, new_ref, cache_ref, out_ref, spill_ref, table_ref, scores_ref, both_ref, sems):
+def partial_kernel(chunk, shards, first_ref, got_ref, *refs):
+    *new_refs, cache_ref, out_ref, spill_ref, table_ref, new_ref, scores_ref, both_ref, sem = refs
     count, width = got_ref.shape
     depth = width - LANES
     rows = cache_ref.shape[0]
     extra = new_ref.shape[0]
     to_log2 = LOG2E / math.sqrt(depth)
-    loads = []
-    for start in range(0, rows, chunk):
-        span = pl.ds(start, chunk)
-        loads.append(pltpu.make_async_copy(cache_ref.at[span, :], table_ref.at[span, :], sems.at[start // chunk]))
-        if len(loads) <= 2:
-            loads[-1].start()
+    load = pltpu.make_async_copy(cache_ref, table_ref, sem)
+    load.start()
+    piece = extra // len(new_refs)
+    for n, ref in enumerate(new_refs):
+        new_ref[n * piece:(n + 1) * piece, :] = ref[...]
     pos = as_row(got_ref[:, depth:], 3)
     column, place, slot, spill = plan_positives(pos, first_ref[0].astype(jnp.float32), rows, shards, SIDE)
     spill_ref[0] = spill.astype(jnp.int32)
@@ -126,16 +125,13 @@
     for (start, size), name in zip(spans, names):
         both_ref[count:, start:start + size] = jnp.where(column == name, 1.0, 0.0).astype(jnp.bfloat16)
 
+    load.wait()
     part_count = count // 2
     tops, totals = [], []
     for at_row in (0, part_count):
         mine = slice(at_row, at_row + part_count)
         top = jnp.full((part_count, LANES), -jnp.inf, jnp.float32)
         for (start, size), gone in zip(spans, dead):
-            if at_row == 0 and start < rows:
-                loads[start // chunk].wait()
-                if start // chunk + 2 < len(loads):
-                    loads[start // chunk + 2].start()
             part = lax.dot_general(
                 got_ref[mine, :depth], block_of(start, size), NT, preferred_element_type=jnp.float32
             )
@@ -233,7 +229,7 @@
     pos_score = jnp.sum(own_ref[...].astype(jnp.float32) * positive, axis=1, keepdims=True) * scale
     loss = (top[0] + jnp.log2(total)) * (1.0 / LOG2E) - pos_score
     line, lane = iota((own, LANES), 0), iota((own, LANES), 1)
-    loss_ref[...] = jnp.sum(jnp.where(line == lane, loss, 0.0), axis=0, keepdims=True)
+    loss_ref[...] = jnp.sum(jnp.where(line == lane, loss, 0.0), axis=0)[:own]
 
 
 def slots_kernel(got_ref, own_ref, grad_ref, loss_ref):
@@ -271,51 +267,57 @@
 
     vmem = pl.BlockSpec(memory_space=pltpu.VMEM)
     smem = pl.BlockSpec(memory_space=pltpu.SMEM)
-    sent = pl.pallas_call(
-        functools.partial(sent_kernel, 3),
-        out_shape=pltpu.VMEM((shards, own, depth + LANES), jnp.bfloat16),
-        in_specs=[smem, vmem], out_specs=vmem,
-    )(positives, queries)
-    got = lax.all_to_all(sent, every, 0, 0, axis_index_groups=plane).reshape(count, depth + LANES)
-
-    new = with_digits(fresh, slots - first, 2)
-    for bit in (1, 4, 2):
-        other = lax.ppermute(new, "group", [(i, i ^ bit) for i in range(groups)])
-        new = jnp.concatenate([new, other], axis=0)
-
+    start = first.reshape(1).astype(jnp.int32)
+    wide = depth + LANES
+    sent, new = pl.pallas_call(
+        sent_kernel,
+        out_shape=(
+            jax.ShapeDtypeStruct((shards, own, wide), jnp.bfloat16),
+            jax.ShapeDtypeStruct((fresh.shape[0], wide), jnp.bfloat16),
+        ),
+        in_specs=[smem, smem, smem, vmem, vmem], out_specs=(vmem, vmem),
+    )(start, positives, slots, queries, fresh)
+    got = lax.all_to_all(sent, every, 0, 0, axis_index_groups=plane).reshape(count, wide)
+    pair = jnp.concatenate([new, lax.ppermute(new, "group", [(i, i ^ 1) for i in range(groups)])], axis=0)
+    pieces = [pair] + [
+        lax.ppermute(pair, "group", [(i, (i + 2 * k) % groups) for i in range(groups)])
+        for k in range(1, groups // 2)
+    ]
+    extra = groups * fresh.shape[0]
     block = count // SIDE
     width = 2 * depth + LANES
     part, spill = pl.pallas_call(
         functools.partial(partial_kernel, CHUNK, shards),
         out_shape=(
-            pltpu.VMEM((SIDE, block + TAIL, depth), jnp.bfloat16),
+            jax.ShapeDtypeStruct((SIDE, block + TAIL, depth), jnp.bfloat16),
             jax.ShapeDtypeStruct((1,), jnp.int32),
         ),
-        in_specs=[smem, vmem, vmem, pl.BlockSpec(memory_space=pl.ANY)],
+        in_specs=[smem, vmem] + [vmem] * len(pieces) + [pl.BlockSpec(memory_space=pl.ANY)],
         out_specs=(vmem, smem),
         scratch_shapes=[
             pltpu.VMEM((rows, depth), jnp.bfloat16),
-            pltpu.VMEM((count, rows + new.shape[0]), jnp.float32),
-            pltpu.VMEM((count + PACKED, rows + new.shape[0]), jnp.bfloat16),
-            pltpu.SemaphoreType.DMA((rows // CHUNK,)),
+            pltpu.VMEM((extra, wide), jnp.bfloat16),
+            pltpu.VMEM((count, rows + extra), jnp.float32),
+            pltpu.VMEM((count + PACKED, rows + extra), jnp.bfloat16),
+            pltpu.SemaphoreType.DMA,
         ],
         compiler_params=pltpu.CompilerParams(vmem_limit_bytes=48 * 1024 * 1024),
         cost_estimate=pl.CostEstimate(
             flops=4 * count * rows * depth, bytes_accessed=2 * rows * depth, transcendentals=count * rows
         ),
-    )(first.reshape(1).astype(jnp.int32), got, new, cache)
+    )(start, got, *pieces, cache)
 
     part = lax.all_to_all(part, every, 0, 0, axis_index_groups=first_ring)
     part = pl.pallas_call(
         block_kernel,
-        out_shape=pltpu.VMEM((block, width), jnp.bfloat16),
+        out_shape=jax.ShapeDtypeStruct((block, width), jnp.bfloat16),
         in_specs=[vmem], out_specs=vmem,
         compiler_params=pltpu.CompilerParams(vmem_limit_bytes=32 * 1024 * 1024),
     )(part)
     back = lax.all_to_all(part.reshape(SIDE, own, width), every, 0, 0, axis_index_groups=second_ring)
     outs = (
         jax.ShapeDtypeStruct((own, depth), jnp.float32),
-        jax.ShapeDtypeStruct((1, LANES), jnp.float32),
+        jax.ShapeDtypeStruct((own,), jnp.float32),
     )
     params = pltpu.CompilerParams(vmem_limit_bytes=32 * 1024 * 1024)
 
@@ -326,6 +328,7 @@
         )(back, queries)
 
     def from_rows():
+        new = jnp.concatenate(pieces, axis=0)
         digits = got[:, depth:depth + 3].astype(jnp.int32)
         local = digits[:, 0] + 256 * digits[:, 1] + 65536 * digits[:, 2] - first
         at = new[:, depth:depth + 2].astype(jnp.int32)
@@ -344,7 +347,7 @@
         )(back, queries, positive)
 
     grad, loss = lax.cond(spill[0] > 0, from_rows, from_slots)
-    return grad, loss[0, :own]
+    return grad, loss
 
 
 def solution(mesh):

time: 94.7 us -> 94.1 us (level)
  starting transfers between devices: 28 us -> 31.7 us
  other arithmetic: 3.67 us -> 0 us
    ppermute x3 -> x4, waiting for transfers between devices: 9.36 us -> 2.82 us  [the longest x3 2.19 us: per_device(): lax.ppermute(pair, 'group', [(i, (i + 2 * k) % groups) for i in range(gro...]
    all_to_all x1, waiting for transfers between devices: 5.48 us -> 11.3 us  [per_device(): lax.all_to_all(sent, every, 0, 0, axis_index_groups=plane)]
    ppermute x3 -> x4, starting transfers between devices: 7.95 us -> 11.7 us  [the longest x3 9.75 us: per_device(): lax.ppermute(pair, 'group', [(i, (i + 2 * k) % groups) for i in range(gro...]
    concatenate x4 -> x0, other arithmetic: 2.99 us -> none  [the longest x3 2.25 us: per_device(): new = jnp.concatenate([new, other], axis=0)]
  transfers between devices with their start and end apart: 5 -> 6, of which waited for: 5 -> 5; matrix products, arithmetic and copies ran while one was open for 4% -> 1% of each run, Pallas kernels for 0% -> 0%
where the time goes in v4:
time: 94.1 us; the launch traced here: 93.5 us
  starting transfers between devices  31.7 us (34%)
  waiting for transfers between devices  23.3 us (25%)
  blocking collectives  22.7 us (24%)
  Pallas kernels  13.7 us (15%)
  between operations  1.35 us (1%)
    all_to_all x1, blocking collectives, per_device(): part = lax.all_to_all(part, every, 0, 0, axis_index_groups=first_ring)  22.7 us
    all_to_all x1, starting transfers between devices, per_device(): lax.all_to_all(sent, every, 0, 0, axis_index_groups=plane)  16.6 us
    all_to_all x1, waiting for transfers between devices, per_device(): lax.all_to_all(sent, every, 0, 0, axis_index_groups=plane)  11.3 us
    pallas_call x1, Pallas kernels, per_device(): pl.pallas_call(functools.partial(partial_kernel, CHUNK, shards), out_shap...  10 us
    ppermute x3, starting transfers between devices, per_device(): lax.ppermute(pair, 'group', [(i, (i + 2 * k) % groups) for i in range(gro...  9.75 us
    all_to_all x1, waiting for transfers between devices, per_device(): lax.all_to_all(part.reshape(SIDE, own, width), every, 0, 0, axis_index_gr...  9.21 us
    all_to_all x1, starting transfers between devices, per_device(): lax.all_to_all(part.reshape(SIDE, own, width), every, 0, 0, axis_index_gr...  3.4 us
    ppermute x3, waiting for transfers between devices, per_device(): lax.ppermute(pair, 'group', [(i, (i + 2 * k) % groups) for i in range(gro...  2.19 us
  transfers between devices with their start and end apart: 6, of which 5 were waited for; matrix products, arithmetic and copies ran while one was open for 1% of the time, Pallas kernels for 0%

profile of v4, /device:TPU:6, one launch (start us, length us, event | category | flops | bytes accessed | tf_op | source)
XLA Modules:
  0.0 93.5 jit_solution(172005529315331332)
XLA Ops:
  0.6 1.8 %shard_map.72 = (bf16[64,8,896]{2,1,0:T(8,128)(2,1)}, bf16[16,896]{1,0:T(8,128)(2,1)}) custom-call(s32[1]{0:T(128)} %bitcast.4.first_ref, s32[8]{0:T(128)} %pos_ref.1, s32[16]{0:T(128)} %slots_ref.1, bf16[8,768]{1,0:T(8,128)(2,1)} %queries_ref.1, bf16[16,768]{1,0:T(8,128)(2,1)} %fresh_ref.1), custom_call_target="tpu_custom_call" | custom-call | tf_op jit(solution)/shard_map/pallas_call | solution.py:272
  2.4 16.6 %all-to-all-start.1 = ((bf16[64,8,896]{2,1,0:T(8,128)(2,1)}), bf16[64,8,896]{2,1,0:T(8,128)(2,1)S(1)}, u32[]{:S(2)}, u32[]{:S(2)}) async-start(bf16[64,8,896]{2,1,0:T(8,128)(2,1)} %get-tuple-element.39), calls=%async_computation.1 | async-start | bytes 1835008 | tf_op jit(solution)/shard_map/all_to_all | solution.py:280
  19.0 1.9 %collective-permute-start = (bf16[16,896]{1,0:T(8,128)(2,1)}, bf16[16,896]{1,0:T(8,128)(2,1)S(1)}, u32[]{:S(2)}, u32[]{:S(2)}) collective-permute-start(bf16[16,896]{1,0:T(8,128)(2,1)} %get-tuple-element.40), channel_id=1, source_target_pairs={{0,64},{64,0},{128,192},{192,128},{256,320},{320,256},{384,448},{4... | collective-permute-start | bytes 86024 | tf_op jit(solution)/shard_map/ppermute | solution.py:281
  21.0 0.8 constant_dynamic-update-slice_fusion.1
  21.7 0.6 collective-permute-done
  22.4 2.7 %collective-permute-start.3 = (bf16[32,896]{1,0:T(8,128)(2,1)S(1)}, bf16[32,896]{1,0:T(8,128)(2,1)S(1)}, u32[]{:S(2)}, u32[]{:S(2)}) collective-permute-start(bf16[32,896]{1,0:T(8,128)(2,1)S(1)} %constant_dynamic-update-slice_fusion.refs_0_), channel_id=1, source_target_pairs={{0,384},{64,448},{128,0},{192,64},{256,128},{320,192},{384,256},{4... | collective-permute-start | bytes 172040 | tf_op jit(solution)/shard_map/ppermute | solution.py:283
  25.1 3.0 %collective-permute-start.2 = (bf16[32,896]{1,0:T(8,128)(2,1)S(1)}, bf16[32,896]{1,0:T(8,128)(2,1)S(1)}, u32[]{:S(2)}, u32[]{:S(2)}) collective-permute-start(bf16[32,896]{1,0:T(8,128)(2,1)S(1)} %constant_dynamic-update-slice_fusion.refs_0_), channel_id=1, source_target_pairs={{0,256},{64,320},{128,384},{192,448},{256,0},{320,64},{384,128},{4... | collective-permute-start | bytes 172040 | tf_op jit(solution)/shard_map/ppermute | solution.py:283
  28.1 4.0 %collective-permute-start.1 = (bf16[32,896]{1,0:T(8,128)(2,1)S(1)}, bf16[32,896]{1,0:T(8,128)(2,1)S(1)}, u32[]{:S(2)}, u32[]{:S(2)}) collective-permute-start(bf16[32,896]{1,0:T(8,128)(2,1)S(1)} %constant_dynamic-update-slice_fusion.refs_0_), channel_id=1, source_target_pairs={{0,128},{64,192},{128,256},{192,320},{256,384},{320,448},{384,0},{... | collective-permute-start | bytes 172040 | tf_op jit(solution)/shard_map/ppermute | solution.py:283
  32.1 0.0 collective-permute-done.3.refs_3_
  32.1 0.5 collective-permute-done.2.refs_2_
  32.7 1.7 %collective-permute-done.1.refs_1_ = bf16[32,896]{1,0:T(8,128)(2,1)S(1)} collective-permute-done((bf16[32,896]{1,0:T(8,128)(2,1)S(1)}, bf16[32,896]{1,0:T(8,128)(2,1)S(1)}, u32[]{:S(2)}, u32[]{:S(2)}) %collective-permute-start.1) | collective-permute-done | bytes 57376 | tf_op jit(solution)/shard_map/ppermute | solution.py:283
  34.3 11.3 %all-to-all-done.1 = bf16[64,8,896]{2,1,0:T(8,128)(2,1)S(1)} async-done(((bf16[64,8,896]{2,1,0:T(8,128)(2,1)}), bf16[64,8,896]{2,1,0:T(8,128)(2,1)S(1)}, u32[]{:S(2)}, u32[]{:S(2)}) %all-to-all-start.1) | async-done | bytes 917536 | tf_op jit(solution)/shard_map/all_to_all | solution.py:280
  45.6 0.0 copy-start
  45.6 10.0 %shard_map.73 = (bf16[8,80,768]{2,1,0:T(8,128)(2,1)S(1)}, s32[1]{0:T(128)}) custom-call(s32[1]{0:T(128)} %bitcast.4.first_ref, bf16[512,896]{1,0:T(8,128)(2,1)S(1)} %bitcast.10, bf16[32,896]{1,0:T(8,128)(2,1)S(1)} %constant_dynamic-update-slice_fusion.refs_0_, bf16[32,896]{1,0:T(8,128)(2,1)S(1)} %collective-permute-done.1.refs_1_, ...), custom_call_target="tpu_custom_call" | custom-call | flops 4831838208 | bytes 4718592 | tf_op jit(solution)/shard_map/pallas_call | solution.py:289
  55.7 22.7 %all_to_all.20.got_ref = bf16[8,80,768]{2,1,0:T(8,128)(2,1)S(1)} all-to-all(bf16[8,80,768]{2,1,0:T(8,128)(2,1)S(1)} %get-tuple-element.42), channel_id=1, replica_groups={{0,8,16,24,32,40,48,56},{1,9,17,25,33,41,49,57},{2,10,18,26,34,42,50,58..., dimensions={0} | all-to-all | bytes 1966080 | tf_op jit(solution)/shard_map/all_to_all | solution.py:310
  78.3 1.2 %shard_map.74 = bf16[64,1664]{1,0:T(8,128)(2,1)} custom-call(bf16[8,80,768]{2,1,0:T(8,128)(2,1)S(1)} %all_to_all.20.got_ref), custom_call_target="tpu_custom_call" | custom-call | tf_op jit(solution)/shard_map/pallas_call | solution.py:311
  79.5 3.4 %all-to-all-start.3 = ((bf16[8,8,1664]{2,1,0:T(8,128)(2,1)}), bf16[8,8,1664]{2,1,0:T(8,128)(2,1)S(1)}, u32[]{:S(2)}, u32[]{:S(2)}) async-start(bf16[8,8,1664]{2,1,0:T(8,128)(2,1)} %bitcast.7), calls=%async_computation.3 | async-start | bytes 425984 | tf_op jit(solution)/shard_map/all_to_all | solution.py:317
  83.6 9.2 %all-to-all-done.3 = bf16[8,8,1664]{2,1,0:T(8,128)(2,1)S(1)} async-done(((bf16[8,8,1664]{2,1,0:T(8,128)(2,1)}), bf16[8,8,1664]{2,1,0:T(8,128)(2,1)S(1)}, u32[]{:S(2)}, u32[]{:S(2)}) %all-to-all-start.3) | async-done | bytes 213024 | tf_op jit(solution)/shard_map/all_to_all | solution.py:317
  92.8 0.0 copy-done
  92.8 0.7 conditional.1
  92.8 0.7 branch_0_fun.1
  (1 shorter events, 0.0 us)
Async XLA Ops:
  2.4 43.2 %all-to-all-start.1 = ((bf16[64,8,896]{2,1,0:T(8,128)(2,1)}), bf16[64,8,896]{2,1,0:T(8,128)(2,1)S(1)}, u32[]{:S(2)}, u32[]{:S(2)}) async-start(bf16[64,8,896]{2,1,0:T(8,128)(2,1)} %get-tuple-element.39), calls=%async_computation.1 | async-start | bytes 1835008 | tf_op jit(solution)/shard_map/all_to_all | solution.py:280
  19.0 3.3 %collective-permute-start = (bf16[16,896]{1,0:T(8,128)(2,1)}, bf16[16,896]{1,0:T(8,128)(2,1)S(1)}, u32[]{:S(2)}, u32[]{:S(2)}) collective-permute-start(bf16[16,896]{1,0:T(8,128)(2,1)} %get-tuple-element.40), channel_id=1, source_target_pairs={{0,64},{64,0},{128,192},{192,128},{256,320},{320,256},{384,448},{4... | collective-permute-start | bytes 86024 | tf_op jit(solution)/shard_map/ppermute | solution.py:281
  22.4 9.8 %collective-permute-start.3 = (bf16[32,896]{1,0:T(8,128)(2,1)S(1)}, bf16[32,896]{1,0:T(8,128)(2,1)S(1)}, u32[]{:S(2)}, u32[]{:S(2)}) collective-permute-start(bf16[32,896]{1,0:T(8,128)(2,1)S(1)} %constant_dynamic-update-slice_fusion.refs_0_), channel_id=1, source_target_pairs={{0,384},{64,448},{128,0},{192,64},{256,128},{320,192},{384,256},{4... | collective-permute-start | bytes 172040 | tf_op jit(solution)/shard_map/ppermute | solution.py:283
  25.1 7.6 %collective-permute-start.2 = (bf16[32,896]{1,0:T(8,128)(2,1)S(1)}, bf16[32,896]{1,0:T(8,128)(2,1)S(1)}, u32[]{:S(2)}, u32[]{:S(2)}) collective-permute-start(bf16[32,896]{1,0:T(8,128)(2,1)S(1)} %constant_dynamic-update-slice_fusion.refs_0_), channel_id=1, source_target_pairs={{0,256},{64,320},{128,384},{192,448},{256,0},{320,64},{384,128},{4... | collective-permute-start | bytes 172040 | tf_op jit(solution)/shard_map/ppermute | solution.py:283
  28.1 6.2 %collective-permute-start.1 = (bf16[32,896]{1,0:T(8,128)(2,1)S(1)}, bf16[32,896]{1,0:T(8,128)(2,1)S(1)}, u32[]{:S(2)}, u32[]{:S(2)}) collective-permute-start(bf16[32,896]{1,0:T(8,128)(2,1)S(1)} %constant_dynamic-update-slice_fusion.refs_0_), channel_id=1, source_target_pairs={{0,128},{64,192},{128,256},{192,320},{256,384},{320,448},{384,0},{... | collective-permute-start | bytes 172040 | tf_op jit(solution)/shard_map/ppermute | solution.py:283
  45.6 47.2 %copy-start = (bf16[8,768]{1,0:T(8,128)(2,1)S(1)}, bf16[8,768]{1,0:T(8,128)(2,1)}, u32[]{:S(2)}) copy-start(bf16[8,768]{1,0:T(8,128)(2,1)} %queries_ref.1) | copy-start | bytes 36868
  79.5 13.3 %all-to-all-start.3 = ((bf16[8,8,1664]{2,1,0:T(8,128)(2,1)}), bf16[8,8,1664]{2,1,0:T(8,128)(2,1)S(1)}, u32[]{:S(2)}, u32[]{:S(2)}) async-start(bf16[8,8,1664]{2,1,0:T(8,128)(2,1)} %bitcast.7), calls=%async_computation.3 | async-start | bytes 425984 | tf_op jit(solution)/shard_map/all_to_all | solution.py:317

commit v5 on v4

--- a/solution.py
+++ b/solution.py
@@ -87,14 +87,20 @@
     return column, place, slot, spill
 
 
+def stage_kernel(cache_ref, other_ref, staged_ref, sem):
+    copy = pltpu.make_async_copy(cache_ref.at[pl.ds(0, staged_ref.shape[0]), :], staged_ref, sem)
+    copy.start()
+    copy.wait()
+
+
 def partial_kernel(chunk, shards, first_ref, got_ref, *refs):
-    *new_refs, cache_ref, out_ref, spill_ref, table_ref, new_ref, scores_ref, both_ref, sem = refs
+    *new_refs, staged_ref, cache_ref, out_ref, spill_ref, table_ref, new_ref, scores_ref, both_ref, sem = refs
     count, width = got_ref.shape
     depth = width - LANES
     rows = cache_ref.shape[0]
     extra = new_ref.shape[0]
     to_log2 = LOG2E / math.sqrt(depth)
-    load = pltpu.make_async_copy(cache_ref, table_ref, sem)
+    load = pltpu.make_async_copy(cache_ref.at[pl.ds(chunk, rows - chunk), :], table_ref, sem)
     load.start()
     piece = extra // len(new_refs)
     for n, ref in enumerate(new_refs):
@@ -111,7 +117,9 @@
     spans = [(start, chunk) for start in range(0, rows, chunk)] + [(rows, extra)]
 
     def block_of(start, size):
-        return new_ref[:, :depth] if start == rows else table_ref[start:start + size, :]
+        if start == rows:
+            return new_ref[:, :depth]
+        return staged_ref[...] if start == 0 else table_ref[start - chunk:start - chunk + size, :]
 
     names, dead = [], []
     for start, size in spans:
@@ -125,40 +133,60 @@
     for (start, size), name in zip(spans, names):
         both_ref[count:, start:start + size] = jnp.where(column == name, 1.0, 0.0).astype(jnp.bfloat16)
 
-    load.wait()
-    part_count = count // 2
-    tops, totals = [], []
-    for at_row in (0, part_count):
-        mine = slice(at_row, at_row + part_count)
-        top = jnp.full((part_count, LANES), -jnp.inf, jnp.float32)
-        for (start, size), gone in zip(spans, dead):
+    blocks = [[spans[-1], spans[0]]] + [[span] for span in spans[1:-1]]
+    order = dict(zip(spans, range(len(spans))))
+    tops, totals, sums = [], [], []
+
+    def score(g):
+        top = jnp.full((count, LANES), -jnp.inf, jnp.float32)
+        for span in blocks[g]:
+            start, size = span
             part = lax.dot_general(
-                got_ref[mine, :depth], block_of(start, size), NT, preferred_element_type=jnp.float32
+                got_ref[:, :depth], block_of(start, size), NT, preferred_element_type=jnp.float32
             )
+            gone = dead[order[span]]
             if gone is not None:
                 part = jnp.where(gone, -jnp.inf, part)
-            scores_ref[mine, start:start + size] = part
+            scores_ref[:, start:start + size] = part
             for at in range(0, size, LANES):
                 top = jnp.maximum(top, part[:, at:at + LANES])
-        top = jnp.max(top, axis=1, keepdims=True) * to_log2
-        total = jnp.zeros((part_count, LANES), jnp.float32)
-        for start, size in spans:
-            weights = jnp.exp2(scores_ref[mine, start:start + size] * to_log2 - top)
+        tops.append(jnp.max(top, axis=1, keepdims=True) * to_log2)
+
+    def weigh(g):
+        total = jnp.zeros((count, LANES), jnp.float32)
+        for start, size in blocks[g]:
+            weights = jnp.exp2(scores_ref[:, start:start + size] * to_log2 - tops[g])
             for at in range(0, size, LANES):
                 total = total + weights[:, at:at + LANES]
-            both_ref[mine, start:start + size] = weights.astype(jnp.bfloat16)
-        tops.append(top)
-        totals.append(total)
-    top, total = jnp.concatenate(tops, axis=0), jnp.concatenate(totals, axis=0)
-    sums = []
-    for mine in (slice(0, part_count), slice(part_count, count + PACKED)):
-        part = jnp.dot(both_ref[mine, :rows], table_ref[...], preferred_element_type=jnp.float32)
-        sums.append(part + jnp.dot(both_ref[mine, rows:], new_ref[:, :depth], preferred_element_type=jnp.float32))
-    summed = jnp.concatenate(sums, axis=0)
-    total = jnp.sum(total, axis=1, keepdims=True)
-    mean = (summed[:count] / total).astype(jnp.bfloat16)
-
-    packed = summed[count:].astype(jnp.bfloat16)
+            both_ref[:count, start:start + size] = weights.astype(jnp.bfloat16)
+        totals.append(jnp.sum(total, axis=1, keepdims=True))
+
+    def add(g):
+        part = 0.0
+        for start, size in blocks[g]:
+            part = part + jnp.dot(
+                both_ref[:, start:start + size], block_of(start, size), preferred_element_type=jnp.float32
+            )
+        sums.append(part)
+
+    last = len(blocks)
+    for g in range(last + 2):
+        if g == 1:
+            load.wait()
+        if g < last:
+            score(g)
+        if 1 <= g <= last:
+            weigh(g - 1)
+        if g >= 2:
+            add(g - 2)
+    top = functools.reduce(jnp.maximum, tops)
+    shares = [jnp.exp2(part - top) for part in tops]
+    total = sum(part * share for part, share in zip(totals, shares))
+    picked = sum(part[count:] for part in sums)
+    summed = sum(part[:count] * share for part, share in zip(sums, shares))
+    mean = (summed / total).astype(jnp.bfloat16)
+
+    packed = picked.astype(jnp.bfloat16)
     place_row = jnp.broadcast_to(place, (PACKED, LANES)).T[0:1]
     spread = jnp.where(iota((SIDE * TAIL, 1), 0).astype(jnp.float32) == place_row, 1.0, 0.0).astype(jnp.bfloat16)
     spread = jnp.dot(spread, packed, preferred_element_type=jnp.float32)
@@ -283,6 +311,14 @@
         lax.ppermute(pair, "group", [(i, (i + 2 * k) % groups) for i in range(groups)])
         for k in range(1, groups // 2)
     ]
+    anywhere = pl.BlockSpec(memory_space=pl.ANY)
+    staged = pl.pallas_call(
+        stage_kernel,
+        out_shape=pltpu.VMEM((CHUNK, depth), jnp.bfloat16),
+        in_specs=[anywhere, anywhere], out_specs=vmem,
+        scratch_shapes=[pltpu.SemaphoreType.DMA],
+        compiler_params=pltpu.CompilerParams(vmem_limit_bytes=2 * 1024 * 1024),
+    )(cache, pieces[-1])
     extra = groups * fresh.shape[0]
     block = count // SIDE
     width = 2 * depth + LANES
@@ -292,10 +328,10 @@
             jax.ShapeDtypeStruct((SIDE, block + TAIL, depth), jnp.bfloat16),
             jax.ShapeDtypeStruct((1,), jnp.int32),
         ),
-        in_specs=[smem, vmem] + [vmem] * len(pieces) + [pl.BlockSpec(memory_space=pl.ANY)],
+        in_specs=[smem, vmem] + [vmem] * (len(pieces) + 1) + [anywhere],
         out_specs=(vmem, smem),
         scratch_shapes=[
-            pltpu.VMEM((rows, depth), jnp.bfloat16),
+            pltpu.VMEM((rows - CHUNK, depth), jnp.bfloat16),
             pltpu.VMEM((extra, wide), jnp.bfloat16),
             pltpu.VMEM((count, rows + extra), jnp.float32),
             pltpu.VMEM((count + PACKED, rows + extra), jnp.bfloat16),
@@ -305,7 +341,7 @@
         cost_estimate=pl.CostEstimate(
             flops=4 * count * rows * depth, bytes_accessed=2 * rows * depth, transcendentals=count * rows
         ),
-    )(start, got, *pieces, cache)
+    )(start, got, *pieces, staged, cache)
 
     part = lax.all_to_all(part, every, 0, 0, axis_index_groups=first_ring)
     part = pl.pallas_call(

time: 94.1 us -> 93.2 us (level)
    ppermute x3, waiting for transfers between devices: 2.19 us -> 0.76 us  [per_device(): lax.ppermute(pair, 'group', [(i, (i + 2 * k) % groups) for i in range(gro...]
    pallas_call x0 -> x1, Pallas kernels: none -> 1.42 us  [per_device(): pl.pallas_call(stage_kernel, out_shape=pltpu.VMEM((CHUNK, depth), jnp.bfl...]
    pallas_call x1, Pallas kernels: 10 us -> 8.84 us  [per_device(): pl.pallas_call(functools.partial(partial_kernel, CHUNK, shards), out_shap...]
  transfers between devices with their start and end apart: 6 -> 6, of which waited for: 5 -> 4; matrix products, arithmetic and copies ran while one was open for 1% -> 0% of each run, Pallas kernels for 0% -> 2%
where the time goes in v5:
time: 93.2 us; the launch traced here: 92.5 us
  starting transfers between devices  31.8 us (34%)
  blocking collectives  22.7 us (24%)
  waiting for transfers between devices  22.6 us (24%)
  Pallas kernels  14 us (15%)
  between operations  1.39 us (1%)
    all_to_all x1, blocking collectives, per_device(): part = lax.all_to_all(part, every, 0, 0, axis_index_groups=first_ring)  22.7 us
    all_to_all x1, starting transfers between devices, per_device(): lax.all_to_all(sent, every, 0, 0, axis_index_groups=plane)  16.7 us
    all_to_all x1, waiting for transfers between devices, per_device(): lax.all_to_all(sent, every, 0, 0, axis_index_groups=plane)  11.5 us
    ppermute x3, starting transfers between devices, per_device(): lax.ppermute(pair, 'group', [(i, (i + 2 * k) % groups) for i in range(gro...  9.75 us
    all_to_all x1, waiting for transfers between devices, per_device(): lax.all_to_all(part.reshape(SIDE, own, width), every, 0, 0, axis_index_gr...  9.21 us
    pallas_call x1, Pallas kernels, per_device(): pl.pallas_call(functools.partial(partial_kernel, CHUNK, shards), out_shap...  8.84 us
    all_to_all x1, starting transfers between devices, per_device(): lax.all_to_all(part.reshape(SIDE, own, width), every, 0, 0, axis_index_gr...  3.4 us
    ppermute x1, starting transfers between devices, per_device(): lax.ppermute(new, 'group', [(i, i ^ 1) for i in range(groups)])  1.92 us
  transfers between devices with their start and end apart: 6, of which 4 were waited for; matrix products, arithmetic and copies ran while one was open for 0% of the time, Pallas kernels for 2%

profile of v5, /device:TPU:6, one launch (start us, length us, event | category | flops | bytes accessed | tf_op | source)
XLA Modules:
  0.0 92.5 jit_solution(3481302202505570294)
XLA Ops:
  0.6 1.8 %shard_map.72 = (bf16[64,8,896]{2,1,0:T(8,128)(2,1)}, bf16[16,896]{1,0:T(8,128)(2,1)}) custom-call(s32[1]{0:T(128)} %bitcast.4.first_ref, s32[8]{0:T(128)} %pos_ref.1, s32[16]{0:T(128)} %slots_ref.1, bf16[8,768]{1,0:T(8,128)(2,1)} %queries_ref.1, bf16[16,768]{1,0:T(8,128)(2,1)} %fresh_ref.1), custom_call_target="tpu_custom_call" | custom-call | tf_op jit(solution)/shard_map/pallas_call | solution.py:300
  2.4 0.0 copy-start.1
  2.4 16.7 %all-to-all-start.1 = ((bf16[64,8,896]{2,1,0:T(8,128)(2,1)}), bf16[64,8,896]{2,1,0:T(8,128)(2,1)S(1)}, u32[]{:S(2)}, u32[]{:S(2)}) async-start(bf16[64,8,896]{2,1,0:T(8,128)(2,1)} %get-tuple-element.39), calls=%async_computation.1 | async-start | bytes 1835008 | tf_op jit(solution)/shard_map/all_to_all | solution.py:308
  19.2 0.0 copy-done.1
  19.2 1.9 %collective-permute-start = (bf16[16,896]{1,0:T(8,128)(2,1)S(1)}, bf16[16,896]{1,0:T(8,128)(2,1)S(1)}, u32[]{:S(2)}, u32[]{:S(2)}) collective-permute-start(bf16[16,896]{1,0:T(8,128)(2,1)S(1)} %copy-done.1), channel_id=1, source_target_pairs={{0,64},{64,0},{128,192},{192,128},{256,320},{320,256},{384,448},{4... | collective-permute-start | bytes 86024 | tf_op jit(solution)/shard_map/ppermute | solution.py:309
  21.1 1.2 %collective-permute-done = bf16[16,896]{1,0:T(8,128)(2,1)S(1)} collective-permute-done((bf16[16,896]{1,0:T(8,128)(2,1)S(1)}, bf16[16,896]{1,0:T(8,128)(2,1)S(1)}, u32[]{:S(2)}, u32[]{:S(2)}) %collective-permute-start) | collective-permute-done | bytes 28704 | tf_op jit(solution)/shard_map/ppermute | solution.py:309
  22.3 2.7 %collective-permute-start.3 = (bf16[32,896]{1,0:T(8,128)(2,1)S(1)}, bf16[32,896]{1,0:T(8,128)(2,1)S(1)}, u32[]{:S(2)}, u32[]{:S(2)}) collective-permute-start(bf16[32,896]{1,0:T(8,128)(2,1)S(1)} %constant_dynamic-update-slice_fusion.refs_0_), channel_id=1, source_target_pairs={{0,384},{64,448},{128,0},{192,64},{256,128},{320,192},{384,256},{4... | collective-permute-start | bytes 172040 | tf_op jit(solution)/shard_map/ppermute | solution.py:311
  25.0 3.0 %collective-permute-start.2 = (bf16[32,896]{1,0:T(8,128)(2,1)S(1)}, bf16[32,896]{1,0:T(8,128)(2,1)S(1)}, u32[]{:S(2)}, u32[]{:S(2)}) collective-permute-start(bf16[32,896]{1,0:T(8,128)(2,1)S(1)} %constant_dynamic-update-slice_fusion.refs_0_), channel_id=1, source_target_pairs={{0,256},{64,320},{128,384},{192,448},{256,0},{320,64},{384,128},{4... | collective-permute-start | bytes 172040 | tf_op jit(solution)/shard_map/ppermute | solution.py:311
  28.0 4.0 %collective-permute-start.1 = (bf16[32,896]{1,0:T(8,128)(2,1)S(1)}, bf16[32,896]{1,0:T(8,128)(2,1)S(1)}, u32[]{:S(2)}, u32[]{:S(2)}) collective-permute-start(bf16[32,896]{1,0:T(8,128)(2,1)S(1)} %constant_dynamic-update-slice_fusion.refs_0_), channel_id=1, source_target_pairs={{0,128},{64,192},{128,256},{192,320},{256,384},{320,448},{384,0},{... | collective-permute-start | bytes 172040 | tf_op jit(solution)/shard_map/ppermute | solution.py:311
  32.1 0.0 collective-permute-done.3.other_ref.refs_3_
  32.1 1.4 %shard_map.73.refs_4_ = bf16[1024,768]{1,0:T(8,128)(2,1)S(1)} custom-call(bf16[3072,768]{1,0:T(8,128)(2,1)} %refs_5_.1, bf16[32,896]{1,0:T(8,128)(2,1)S(1)} %collective-permute-done.3.other_ref.refs_3_), custom_call_target="tpu_custom_call" | custom-call | tf_op jit(solution)/shard_map/pallas_call | solution.py:315
  33.5 0.0 collective-permute-done.2.refs_2_
  33.5 0.8 collective-permute-done.1.refs_1_
  34.3 11.5 %all-to-all-done.1 = bf16[64,8,896]{2,1,0:T(8,128)(2,1)S(1)} async-done(((bf16[64,8,896]{2,1,0:T(8,128)(2,1)}), bf16[64,8,896]{2,1,0:T(8,128)(2,1)S(1)}, u32[]{:S(2)}, u32[]{:S(2)}) %all-to-all-start.1) | async-done | bytes 917536 | tf_op jit(solution)/shard_map/all_to_all | solution.py:308
  45.8 8.8 %shard_map.74 = (bf16[8,80,768]{2,1,0:T(8,128)(2,1)S(1)}, s32[1]{0:T(128)}) custom-call(s32[1]{0:T(128)} %bitcast.4.first_ref, bf16[512,896]{1,0:T(8,128)(2,1)S(1)} %bitcast.10, bf16[32,896]{1,0:T(8,128)(2,1)S(1)} %constant_dynamic-update-slice_fusion.refs_0_, bf16[32,896]{1,0:T(8,128)(2,1)S(1)} %collective-permute-done.1.refs_1_, ...), custom_call_target="tpu_custom_call" | custom-call | flops 4831838208 | bytes 4718592 | tf_op jit(solution)/shard_map/pallas_call | solution.py:325
  54.6 0.0 copy-start
  54.6 22.7 %all_to_all.20.got_ref = bf16[8,80,768]{2,1,0:T(8,128)(2,1)S(1)} all-to-all(bf16[8,80,768]{2,1,0:T(8,128)(2,1)S(1)} %get-tuple-element.42), channel_id=1, replica_groups={{0,8,16,24,32,40,48,56},{1,9,17,25,33,41,49,57},{2,10,18,26,34,42,50,58..., dimensions={0} | all-to-all | bytes 1966080 | tf_op jit(solution)/shard_map/all_to_all | solution.py:346
  77.3 1.2 %shard_map.75 = bf16[64,1664]{1,0:T(8,128)(2,1)} custom-call(bf16[8,80,768]{2,1,0:T(8,128)(2,1)S(1)} %all_to_all.20.got_ref), custom_call_target="tpu_custom_call" | custom-call | tf_op jit(solution)/shard_map/pallas_call | solution.py:347
  78.5 3.4 %all-to-all-start.3 = ((bf16[8,8,1664]{2,1,0:T(8,128)(2,1)}), bf16[8,8,1664]{2,1,0:T(8,128)(2,1)S(1)}, u32[]{:S(2)}, u32[]{:S(2)}) async-start(bf16[8,8,1664]{2,1,0:T(8,128)(2,1)} %bitcast.7), calls=%async_computation.3 | async-start | bytes 425984 | tf_op jit(solution)/shard_map/all_to_all | solution.py:353
  82.6 9.2 %all-to-all-done.3 = bf16[8,8,1664]{2,1,0:T(8,128)(2,1)S(1)} async-done(((bf16[8,8,1664]{2,1,0:T(8,128)(2,1)}), bf16[8,8,1664]{2,1,0:T(8,128)(2,1)S(1)}, u32[]{:S(2)}, u32[]{:S(2)}) %all-to-all-start.3) | async-done | bytes 213024 | tf_op jit(solution)/shard_map/all_to_all | solution.py:353
  91.8 0.0 copy-done
  91.8 0.7 conditional.1
  91.8 0.7 branch_0_fun.1
  (2 shorter events, 0.0 us)
Async XLA Ops:
  2.4 16.7 %copy-start.1 = (bf16[16,896]{1,0:T(8,128)(2,1)S(1)}, bf16[16,896]{1,0:T(8,128)(2,1)}, u32[]{:S(2)}) copy-start(bf16[16,896]{1,0:T(8,128)(2,1)} %get-tuple-element.40) | copy-start | bytes 86020
  2.4 43.3 %all-to-all-start.1 = ((bf16[64,8,896]{2,1,0:T(8,128)(2,1)}), bf16[64,8,896]{2,1,0:T(8,128)(2,1)S(1)}, u32[]{:S(2)}, u32[]{:S(2)}) async-start(bf16[64,8,896]{2,1,0:T(8,128)(2,1)} %get-tuple-element.39), calls=%async_computation.1 | async-start | bytes 1835008 | tf_op jit(solution)/shard_map/all_to_all | solution.py:308
  19.2 3.1 %collective-permute-start = (bf16[16,896]{1,0:T(8,128)(2,1)S(1)}, bf16[16,896]{1,0:T(8,128)(2,1)S(1)}, u32[]{:S(2)}, u32[]{:S(2)}) collective-permute-start(bf16[16,896]{1,0:T(8,128)(2,1)S(1)} %copy-done.1), channel_id=1, source_target_pairs={{0,64},{64,0},{128,192},{192,128},{256,320},{320,256},{384,448},{4... | collective-permute-start | bytes 86024 | tf_op jit(solution)/shard_map/ppermute | solution.py:309
  22.3 9.8 %collective-permute-start.3 = (bf16[32,896]{1,0:T(8,128)(2,1)S(1)}, bf16[32,896]{1,0:T(8,128)(2,1)S(1)}, u32[]{:S(2)}, u32[]{:S(2)}) collective-permute-start(bf16[32,896]{1,0:T(8,128)(2,1)S(1)} %constant_dynamic-update-slice_fusion.refs_0_), channel_id=1, source_target_pairs={{0,384},{64,448},{128,0},{192,64},{256,128},{320,192},{384,256},{4... | collective-permute-start | bytes 172040 | tf_op jit(solution)/shard_map/ppermute | solution.py:311
  25.0 8.5 %collective-permute-start.2 = (bf16[32,896]{1,0:T(8,128)(2,1)S(1)}, bf16[32,896]{1,0:T(8,128)(2,1)S(1)}, u32[]{:S(2)}, u32[]{:S(2)}) collective-permute-start(bf16[32,896]{1,0:T(8,128)(2,1)S(1)} %constant_dynamic-update-slice_fusion.refs_0_), channel_id=1, source_target_pairs={{0,256},{64,320},{128,384},{192,448},{256,0},{320,64},{384,128},{4... | collective-permute-start | bytes 172040 | tf_op jit(solution)/shard_map/ppermute | solution.py:311
  28.0 6.2 %collective-permute-start.1 = (bf16[32,896]{1,0:T(8,128)(2,1)S(1)}, bf16[32,896]{1,0:T(8,128)(2,1)S(1)}, u32[]{:S(2)}, u32[]{:S(2)}) collective-permute-start(bf16[32,896]{1,0:T(8,128)(2,1)S(1)} %constant_dynamic-update-slice_fusion.refs_0_), channel_id=1, source_target_pairs={{0,128},{64,192},{128,256},{192,320},{256,384},{320,448},{384,0},{... | collective-permute-start | bytes 172040 | tf_op jit(solution)/shard_map/ppermute | solution.py:311
  54.6 37.2 %copy-start = (bf16[8,768]{1,0:T(8,128)(2,1)S(1)}, bf16[8,768]{1,0:T(8,128)(2,1)}, u32[]{:S(2)}) copy-start(bf16[8,768]{1,0:T(8,128)(2,1)} %queries_ref.1) | copy-start | bytes 36868
  78.5 13.3 %all-to-all-start.3 = ((bf16[8,8,1664]{2,1,0:T(8,128)(2,1)}), bf16[8,8,1664]{2,1,0:T(8,128)(2,1)S(1)}, u32[]{:S(2)}, u32[]{:S(2)}) async-start(bf16[8,8,1664]{2,1,0:T(8,128)(2,1)} %bitcast.7), calls=%async_computation.3 | async-start | bytes 425984 | tf_op jit(solution)/shard_map/all_to_all | solution.py:353
